TPU v7x, 32 devices: a whole 2x2x4 slice. The times are simulated.
32 devices in a mesh: replica: 8 (over y, x, core), shard: 4 (over z).
Axes of the slice: x: 2, y: 2, z: 4, core: 2. Of those that a mesh axis runs over, the one named last changes fastest.
Arguments:
- clips: bfloat16 [16, 256, 1024], P('replica', 'shard'), may hold values from -6 to 6
- cotangent: bfloat16 [16, 256, 1024], P('replica', 'shard'), may hold values from -6 to 6
- live_count: int32 [8], P('replica'), may hold values from 1 to 2, 12 in all
- w_qkv: bfloat16 [1024, 3072], P('shard'), may hold values from -0.1875 to 0.1875
- w_out: bfloat16 [1024, 1024], P('shard'), may hold values from -1.5 to 1.5
- w_fc1: bfloat16 [1024, 4096], P('shard'), may hold values from -0.1875 to 0.1875
- w_fc2: bfloat16 [4096, 1024], P('shard'), may hold values from -0.09375 to 0.09375
- norm_gain: bfloat16 [2, 1024], P(None, 'shard'), may hold values from 0.5 to 1.5
- norm_bias: bfloat16 [2, 1024], P(None, 'shard'), may hold values from -1.796875 to 1.796875
- proj_bias: bfloat16 [4, 1024], P(None, 'shard'), may hold values from -1.796875 to 1.796875
- fc1_bias: bfloat16 [4096], P('shard'), may hold values from -1.796875 to 1.796875
Outputs:
- out: bfloat16 [16, 256, 1024], P('replica', 'shard')
- clips_grad: float32 [16, 256, 1024], P('replica', 'shard')
- w_qkv_grad: float32 [1024, 3072], P('shard')
- w_out_grad: float32 [1024, 1024], P('shard')
- w_fc1_grad: float32 [1024, 4096], P('shard')
- w_fc2_grad: float32 [4096, 1024], P('shard')
- norm_gain_grad: float32 [2, 1024], P(None, 'shard')
- norm_bias_grad: float32 [2, 1024], P(None, 'shard')
- proj_bias_grad: float32 [4, 1024], P(None, 'shard')
- fc1_bias_grad: float32 [4096], P('shard')
Inputs may be any that keep to these rules, and one draw needn't show every extreme that they name: `live_count`: each replica group holds its clips in its first places; some group holds 2, and there are 12 clips in all.
All inputs are finite; a program needn't handle non-finite values.
Results may differ from a plain program's by a relative error of at most 0.0085.
Values may be sent and summed in bfloat16 or wider, within the bound.
A program may use at most 192 MiB of HBM per device.

v0:
```python
import math

import jax
import jax.numpy as jnp
from jax import lax
from jax.sharding import PartitionSpec as P

HEAD_DIM = 64


def layer_normalizer(value):
    centre = value - jnp.mean(value, axis=-1, keepdims=True)
    spread = jnp.mean(centre * centre, axis=-1, keepdims=True)
    inverse_deviation = lax.rsqrt(spread + 1e-06)
    return (centre * inverse_deviation, inverse_deviation)


def norm_backward_step(scaled_gradient, normalized_input, inverse_deviation):
    first_branch = jnp.mean(scaled_gradient, axis=-1, keepdims=True)
    second_branch = jnp.mean(scaled_gradient * normalized_input, axis=-1, keepdims=True)
    return inverse_deviation * (scaled_gradient - first_branch - normalized_input * second_branch)


def to_blocks(tensor):
    slots, count, width = tensor.shape
    halves = tensor.reshape(slots, count, 2, width // 2).transpose(0, 2, 1, 3)
    return halves.reshape(slots * 2, count, width // 2)


def from_blocks(tensor, slots):
    items, count, half = tensor.shape
    joined = tensor.reshape(slots, 2, count, half).transpose(0, 2, 1, 3)
    return joined.reshape(slots, count, 2 * half)


def split_heads(tensor):
    return tensor.reshape(tensor.shape[0], tensor.shape[1] // HEAD_DIM, HEAD_DIM)


def attend_forward(item):
    q_part, k_part, v_part = item
    scale = 1.0 / math.sqrt(HEAD_DIM)
    q_heads = split_heads(q_part)
    k_heads = split_heads(k_part)
    v_heads = split_heads(v_part)
    scores = (
        jnp.einsum("qhd,khd->hqk", q_heads, k_heads, preferred_element_type=jnp.float32) * scale
    )
    top = jnp.max(scores, axis=-1, keepdims=True)
    expo = jnp.exp(scores - top)
    total = jnp.sum(expo, axis=-1, keepdims=True)
    probs = (expo / total).astype(jnp.bfloat16)
    mixed = jnp.einsum("hqk,khd->qhd", probs, v_heads, preferred_element_type=jnp.float32)
    mixed = mixed.reshape(q_part.shape[0], q_part.shape[1]).astype(jnp.bfloat16)
    return (mixed, top[..., 0] + jnp.log(total[..., 0]))


def attend_backward(item):
    q_part, k_part, v_part, d_part, lse = item
    scale = 1.0 / math.sqrt(HEAD_DIM)
    q_heads = split_heads(q_part)
    k_heads = split_heads(k_part)
    v_heads = split_heads(v_part)
    d_heads = split_heads(d_part)
    scores = (
        jnp.einsum("qhd,khd->hqk", q_heads, k_heads, preferred_element_type=jnp.float32) * scale
    )
    probs = jnp.exp(scores - lse[..., None])
    probs_low = probs.astype(jnp.bfloat16)
    d_probs = jnp.einsum("qhd,khd->hqk", d_heads, v_heads, preferred_element_type=jnp.float32)
    inner = jnp.sum(probs * d_probs, axis=-1, keepdims=True)
    d_scores = (probs * (d_probs - inner)).astype(jnp.bfloat16)
    d_query = (
        jnp.einsum("hqk,khd->qhd", d_scores, k_heads, preferred_element_type=jnp.float32) * scale
    )
    d_keys = (
        jnp.einsum("hqk,qhd->khd", d_scores, q_heads, preferred_element_type=jnp.float32) * scale
    )
    d_values = jnp.einsum("hqk,qhd->khd", probs_low, d_heads, preferred_element_type=jnp.float32)
    return (
        d_query.reshape(q_part.shape[0], q_part.shape[1]),
        d_keys.reshape(k_part.shape[0], k_part.shape[1]),
        d_values.reshape(v_part.shape[0], v_part.shape[1]),
    )


def gelu_slope(value):
    cdf = 0.5 * (1.0 + jax.scipy.special.erf(value * (1.0 / math.sqrt(2.0))))
    return cdf + value * jnp.exp(-0.5 * value * value) * (1.0 / math.sqrt(2.0 * math.pi))


def outer_sum(left, right):
    return jnp.einsum("ti,tj->ij", left, right, preferred_element_type=jnp.float32)


def back_product(grad, weight):
    return jnp.einsum("tj,ij->ti", grad, weight, preferred_element_type=jnp.float32)


def local(
    clips,
    cotangent,
    live_count,
    w_qkv,
    w_out,
    w_fc1,
    w_fc2,
    norm_gain,
    norm_bias,
    proj_bias,
    fc1_bias,
):
    slots, rows, width = clips.shape
    shape3 = (slots, rows, width)
    fetched = (
        lax.all_gather(w_qkv, "shard", axis=0, tiled=True),
        lax.all_gather(w_out, "shard", axis=0, tiled=True),
        lax.all_gather(w_fc1, "shard", axis=0, tiled=True),
        lax.all_gather(w_fc2, "shard", axis=0, tiled=True),
        lax.all_gather(norm_gain, "shard", axis=1, tiled=True),
        lax.all_gather(norm_bias, "shard", axis=1, tiled=True),
        lax.all_gather(proj_bias, "shard", axis=1, tiled=True),
        lax.all_gather(fc1_bias, "shard", axis=0, tiled=True),
    )
    wq_full, wo_full, w1_full, w2_full, gains_low, nbias_low, pbias_low, fbias_low = fetched
    gain_vectors = gains_low.astype(jnp.float32)
    norm_shift_bias = nbias_low.astype(jnp.float32)
    pbias = pbias_low.astype(jnp.float32)
    fbias = fbias_low.astype(jnp.float32)
    flattened_rows = clips.reshape(slots * rows, width).astype(jnp.float32)
    first_normalized_input, first_inverse_deviation = layer_normalizer(flattened_rows)
    first_branch = (first_normalized_input * gain_vectors[0] + norm_shift_bias[0]).astype(
        jnp.bfloat16
    )
    joint = jnp.dot(first_branch, wq_full, preferred_element_type=jnp.float32)
    query = (joint[:, :width] + pbias[0]).astype(jnp.bfloat16).reshape(shape3)
    keys = joint[:, width : 2 * width].astype(jnp.bfloat16).reshape(shape3)
    values = (joint[:, 2 * width :] + pbias[1]).astype(jnp.bfloat16).reshape(shape3)
    keys_all, values_all = (
        lax.all_gather(keys, "shard", axis=1, tiled=True),
        lax.all_gather(values, "shard", axis=1, tiled=True),
    )
    q_blocks = to_blocks(query)
    mixed_blocks, lse = lax.map(
        attend_forward, (q_blocks, to_blocks(keys_all), to_blocks(values_all))
    )
    mixed = from_blocks(mixed_blocks, slots).reshape(slots * rows, width)
    branch = jnp.dot(mixed, wo_full, preferred_element_type=jnp.float32) + pbias[2]
    residual_stream = flattened_rows + branch
    second_normalized_input, second_inverse_deviation = layer_normalizer(residual_stream)
    second_branch = (second_normalized_input * gain_vectors[1] + norm_shift_bias[1]).astype(
        jnp.bfloat16
    )
    pre = jnp.dot(second_branch, w1_full, preferred_element_type=jnp.float32) + fbias
    act = jax.nn.gelu(pre, approximate=False).astype(jnp.bfloat16)
    mlp = jnp.dot(act, w2_full, preferred_element_type=jnp.float32) + pbias[3]
    alive = (jnp.arange(slots, dtype=jnp.int32) < live_count[0]).astype(jnp.float32)
    row_mask = jnp.repeat(alive, rows)[:, None]
    out = ((residual_stream + mlp) * row_mask).astype(jnp.bfloat16).reshape(shape3)
    wq_back, wo_back, w1_back, w2_back = (
        lax.all_gather(w_qkv, "shard", axis=0, tiled=True),
        lax.all_gather(w_out, "shard", axis=0, tiled=True),
        lax.all_gather(w_fc1, "shard", axis=0, tiled=True),
        lax.all_gather(w_fc2, "shard", axis=0, tiled=True),
    )
    output_gradient = cotangent.reshape(slots * rows, width).astype(jnp.float32) * row_mask
    d_mlp = output_gradient.astype(jnp.bfloat16)
    d_fc2_bias = jnp.sum(d_mlp.astype(jnp.float32), axis=0)
    d_w2 = outer_sum(act, d_mlp)
    d_act = back_product(d_mlp, w2_back)
    d_pre = (d_act * gelu_slope(pre)).astype(jnp.bfloat16)
    d_fbias = jnp.sum(d_pre.astype(jnp.float32), axis=0)
    d_w1 = outer_sum(second_branch, d_pre)
    second_branch_gradient = back_product(d_pre, w1_back)
    second_gain_gradient = jnp.sum(second_branch_gradient * second_normalized_input, axis=0)
    d_nbias_two = jnp.sum(second_branch_gradient, axis=0)
    residual_gradient = output_gradient + norm_backward_step(
        second_branch_gradient * gain_vectors[1], second_normalized_input, second_inverse_deviation
    )
    d_branch = residual_gradient.astype(jnp.bfloat16)
    d_out_bias = jnp.sum(d_branch.astype(jnp.float32), axis=0)
    d_wo = outer_sum(mixed, d_branch)
    d_mixed = back_product(d_branch, wo_back).astype(jnp.bfloat16).reshape(shape3)
    keys_back, values_back = (keys_all, values_all)
    dq_blocks, dk_blocks, dv_blocks = lax.map(
        attend_backward,
        (q_blocks, to_blocks(keys_back), to_blocks(values_back), to_blocks(d_mixed), lse),
    )
    dk_part = from_blocks(dk_blocks, slots)
    dv_part = from_blocks(dv_blocks, slots)
    dk_own, dv_own = (
        lax.psum_scatter(dk_part, "shard", scatter_dimension=1, tiled=True),
        lax.psum_scatter(dv_part, "shard", scatter_dimension=1, tiled=True),
    )
    d_query = from_blocks(dq_blocks, slots).reshape(slots * rows, width).astype(jnp.bfloat16)
    d_keys = dk_own.reshape(slots * rows, width).astype(jnp.bfloat16)
    d_values = dv_own.reshape(slots * rows, width).astype(jnp.bfloat16)
    d_joint = jnp.concatenate([d_query, d_keys, d_values], axis=1)
    d_q_bias = jnp.sum(d_query.astype(jnp.float32), axis=0)
    d_v_bias = jnp.sum(d_values.astype(jnp.float32), axis=0)
    d_wq = outer_sum(first_branch, d_joint)
    first_branch_gradient = back_product(d_joint, wq_back)
    first_gain_gradient = jnp.sum(first_branch_gradient * first_normalized_input, axis=0)
    d_nbias_one = jnp.sum(first_branch_gradient, axis=0)
    input_gradient = residual_gradient + norm_backward_step(
        first_branch_gradient * gain_vectors[0], first_normalized_input, first_inverse_deviation
    )
    clips_grad = input_gradient.reshape(shape3)
    d_gains = jnp.stack([first_gain_gradient, second_gain_gradient])
    d_nbias = jnp.stack([d_nbias_one, d_nbias_two])
    d_pbias = jnp.stack([d_q_bias, d_v_bias, d_out_bias, d_fc2_bias])
    owned = (
        lax.psum_scatter(d_wq, "shard", scatter_dimension=0, tiled=True),
        lax.psum_scatter(d_wo, "shard", scatter_dimension=0, tiled=True),
        lax.psum_scatter(d_w1, "shard", scatter_dimension=0, tiled=True),
        lax.psum_scatter(d_w2, "shard", scatter_dimension=0, tiled=True),
        lax.psum_scatter(d_gains, "shard", scatter_dimension=1, tiled=True),
        lax.psum_scatter(d_nbias, "shard", scatter_dimension=1, tiled=True),
        lax.psum_scatter(d_pbias, "shard", scatter_dimension=1, tiled=True),
        lax.psum_scatter(d_fbias, "shard", scatter_dimension=0, tiled=True),
    )
    summed = lax.psum(
        (owned[0], owned[1], owned[2], owned[3], owned[4], owned[5], owned[6], owned[7]), "replica"
    )
    return (
        out,
        clips_grad,
        summed[0],
        summed[1],
        summed[2],
        summed[3],
        summed[4],
        summed[5],
        summed[6],
        summed[7],
    )


def solution(mesh):
    in_specs = (
        P("replica", "shard", None),
        P("replica", "shard", None),
        P("replica"),
        P("shard", None),
        P("shard", None),
        P("shard", None),
        P("shard", None),
        P(None, "shard"),
        P(None, "shard"),
        P(None, "shard"),
        P("shard"),
    )
    out_specs = (
        P("replica", "shard", None),
        P("replica", "shard", None),
        P("shard", None),
        P("shard", None),
        P("shard", None),
        P("shard", None),
        P(None, "shard"),
        P(None, "shard"),
        P(None, "shard"),
        P("shard"),
    )
    return jax.shard_map(local, mesh=mesh, in_specs=in_specs, out_specs=out_specs, check_vma=False)
```

profile of v0, /device:TPU:0, one launch (start us, length us, event | category | flops | bytes accessed | tf_op | source)
XLA Modules:
  0.0 1790.8 jit_solution(999356061080632260)
XLA Ops:
  8.0 1.1 convert_reduce_fusion.5
  9.2 1.2 multiply_reduce_fusion.6
  10.4 12.6 all_gather.35
  23.0 7.7 all_gather.34
  30.8 14.0 all_gather.37
  45.1 82.8 %all-gather.7.cloned.1.call-done = bf16[1024,3072]{1,0:T(8,128)(2,1)} async-done(((bf16[256,3072]{1,0:T(8,128)(2,1)}), bf16[1024,3072]{1,0:T(8,128)(2,1)}) %all-gather.7.cloned.1.call-update) | async-done | bytes 6291472 | tf_op jit(solution)/shard_map/all_gather | solution.py:116
  127.9 3.8 fusion.45
  135.2 12.0 all_gather.42
  149.1 9.8 all-gather.9.cloned.1.call-done
  158.9 1.3 fusion.39
  161.0 27.5 %all-gather.11.cloned.1.call-done = bf16[2,256,1024]{2,1,0:T(8,128)(2,1)} async-done(((bf16[2,64,1024]{2,1,0:T(8,128)(2,1)}), bf16[2,256,1024]{2,1,0:T(8,128)(2,1)}) %all-gather.11.cloned.1.call-update) | async-done | bytes 1048592 | tf_op jit(solution)/shard_map/all_gather | solution.py:140
  188.5 1.3 fusion.38
  189.8 1.3 copy.62
  191.2 11.1 while.26
  191.2 1.0 constant_dynamic-slice_fusion.13
  193.9 1.0 constant_dynamic-slice_fusion.13
  196.7 1.0 constant_dynamic-slice_fusion.13
  199.5 1.0 constant_dynamic-slice_fusion.13
  202.3 1.4 copy.63
  203.7 31.7 %all-gather.13.cloned.1.call-done = bf16[1024,1024]{1,0:T(8,128)(2,1)} async-done(((bf16[256,1024]{1,0:T(8,128)(2,1)}), bf16[1024,1024]{1,0:T(8,128)(2,1)}) %all-gather.13.cloned.1.call-update) | async-done | bytes 2097168 | tf_op jit(solution)/shard_map/all_gather | solution.py:117
  235.4 2.1 fusion.43
  237.7 147.4 %all-gather.15.cloned.1.call-done = bf16[1024,4096]{1,0:T(8,128)(2,1)} async-done(((bf16[256,4096]{1,0:T(8,128)(2,1)}), bf16[1024,4096]{1,0:T(8,128)(2,1)}) %all-gather.15.cloned.1.call-update) | async-done | bytes 8388624 | tf_op jit(solution)/shard_map/all_gather | solution.py:118
  385.1 9.3 fusion.9
  394.4 140.0 %all-gather.17.cloned.1.call-done = bf16[4096,1024]{1,0:T(8,128)(2,1)} async-done(((bf16[1024,1024]{1,0:T(8,128)(2,1)}), bf16[4096,1024]{1,0:T(8,128)(2,1)}) %all-gather.17.cloned.1.call-update) | async-done | bytes 8388624 | tf_op jit(solution)/shard_map/all_gather | solution.py:119
  534.4 7.2 convert_reduce_fusion
  541.7 3.0 multiply_reduce_fusion.1
  546.8 24.6 %while.27 = (s32[]{:T(128)}, bf16[4,64,512]{1,2,0:T(8,128)(2,1)}, f32[4,256,512]{1,2,0:T(8,128)}, f32[4,256,512]{1,2,0:T(8,128)}, bf16[4,256,512]{1,2,0:T(8,128)...) while((s32[]{:T(128)}, bf16[4,64,512]{1,2,0:T(8,128)(2,1)}, ...), condition=%wide.region_12.13_spmd, body=%wide.region_10.12_spmd.sunk | while | flops 85130752 | bytes 9971849 | solution.py:185
  551.9 1.0 constant_dynamic-update-slice_fusion.9
  558.1 1.0 constant_dynamic-update-slice_fusion.9
  564.2 1.0 constant_dynamic-update-slice_fusion.9
  570.3 1.0 constant_dynamic-update-slice_fusion.9
  571.4 2.9 copy.68
  574.3 2.9 reshape.226
  577.2 2.9 copy.69
  580.1 2.8 reshape.228
  583.8 2.7 fusion.33
  587.9 31.4 %reduce-scatter.16.cloned.1.call-done = f32[2,64,1024]{2,1,0:T(8,128)} async-done(((f32[2,256,1024]{2,1,0:T(8,128)}), f32[2,64,1024]{2,1,0:T(8,128)}) %reduce-scatter.16.cloned.1.call-update) | async-done | bytes 524304 | tf_op jit(solution)/shard_map/reduce_scatter | solution.py:192
  619.3 1.1 convert_element_type.165
  620.4 45.2 %reduce-scatter.18.cloned.1.call-done = f32[2,64,1024]{2,1,0:T(8,128)} async-done(((f32[2,256,1024]{2,1,0:T(8,128)}), f32[2,64,1024]{2,1,0:T(8,128)}) %reduce-scatter.18.cloned.1.call-update) | async-done | bytes 524304 | tf_op jit(solution)/shard_map/reduce_scatter | solution.py:193
  665.6 1.1 convert_reduce_fusion.4
  666.7 6.3 fusion.29
  673.1 1.5 copy-done.5
  674.5 8.2 fusion.36
  682.8 1.2 copy-done
  684.0 8.1 fusion.46
  693.5 5.4 multiply_reduce_fusion.2
  698.9 1.0 copy.70
  700.3 1.0 copy.72
  701.4 1.0 copy.74
  702.5 42.1 %reduce-scatter.22.cloned.1.call-done = f32[256,1024]{1,0:T(8,128)} async-done(((f32[1024,1024]{1,0:T(8,128)}), f32[256,1024]{1,0:T(8,128)}) %reduce-scatter.22.cloned.1.call-update) | async-done | bytes 1048592 | tf_op jit(solution)/shard_map/reduce_scatter | solution.py:214
  744.6 214.7 %reduce-scatter.20.cloned.1.call-done = f32[256,3072]{1,0:T(8,128)} async-done(((f32[1024,3072]{1,0:T(8,128)}), f32[256,3072]{1,0:T(8,128)}) %reduce-scatter.20.cloned.1.call-update) | async-done | bytes 3145744 | tf_op jit(solution)/shard_map/reduce_scatter | solution.py:213
  959.3 283.9 %reduce-scatter.24.cloned.1.call-done = f32[256,4096]{1,0:T(8,128)} async-done(((f32[1024,4096]{1,0:T(8,128)}), f32[256,4096]{1,0:T(8,128)}) %reduce-scatter.24.cloned.1.call-update) | async-done | bytes 4194320 | tf_op jit(solution)/shard_map/reduce_scatter | solution.py:215
  1243.2 283.3 %reduce-scatter.26.cloned.1.call-done = f32[1024,1024]{1,0:T(8,128)} async-done(((f32[4096,1024]{1,0:T(8,128)}), f32[1024,1024]{1,0:T(8,128)}) %reduce-scatter.26.cloned.1.call-update) | async-done | bytes 4194320 | tf_op jit(solution)/shard_map/reduce_scatter | solution.py:216
  1528.3 18.4 %all-reduce = f32[4096]{0:T(1024)S(1)} all-reduce(f32[4096]{0:T(1024)S(1)} %get-tuple-element.220), channel_id=11, replica_groups=mesh['replica'=8,'shard'=4] {'shard'}, use_global_device_ids=true, to_apply=%region_41.42.clone | all-reduce | flops 4096 | bytes 32768
  1546.8 5.4 fusion.24
  1552.2 1.0 multiply_add_fusion
  1554.2 20.3 %reduce-scatter.30.cloned.1.call-done = f32[256,2]{1,0:T(8,128)} async-done(((f32[1024,2]{1,0:T(8,128)}), f32[256,2]{1,0:T(8,128)}) %reduce-scatter.30.cloned.1.call-update) | async-done | bytes 2064
  1575.5 21.8 %reduce-scatter.32.cloned.1.call-done = f32[256,4]{1,0:T(8,128)} async-done(((f32[1024,4]{1,0:T(8,128)}), f32[256,4]{1,0:T(8,128)}) %reduce-scatter.32.cloned.1.call-update) | async-done | bytes 4112
  1598.3 23.2 %all-reduce.1 = (f32[2,256]{1,0:T(2,128)}, f32[2,256]{1,0:T(2,128)}, f32[4,256]{1,0:T(4,128)}, f32[1024]{0:T(1024)}) all-reduce(f32[2,256]{1,0:T(2,128)S(1)} %copy.71, f32[2,256]{1,0:T(2,128)S(1)} %copy.73, f32[4,256]{1,0:T(4,128)S(1)} %copy.75, f32[1024]{0:T(1024)S(1)} %dynamic-slice-done), channel_id=1, replica_groups=mesh['replica'=8,'shard'=4] {'replica'}, use_global_device_ids=true, to_apply=%region_28.29 | all-reduce | flops 3072 | bytes 24576 | tf_op jit(solution)/shard_map/psum | solution.py:222
  1621.5 152.0 %all-reduce.5.cloned.1.call-done = (f32[256,3072]{1,0:T(8,128)}, f32[256,1024]{1,0:T(8,128)}, f32[256,4096]{1,0:T(8,128)}, f32[1024,1024]{1,0:T(8,128)}) async-done(((f32[256,3072]{1,0:T(8,128)}, f32[256,1024]{1,0:T(8,128)}, f32[256,4096]{1,0:T(8,128)}, f32[1024,1024]{1,0:T(8,128)}), (f32[256,3072]{1,0:T(8,128)}, f32[256,1024]{1,0:T(8,128)}, f32[256,4096]{1,0:T(8,128)}, ...) | async-done | bytes 12582928 | tf_op jit(solution)/shard_map/psum | solution.py:222
  1773.5 4.0 copy.124
  1778.5 2.1 copy.126
  1780.7 1.6 copy-done.6
  1782.2 2.0 copy.127
  (231 shorter events, 45.5 us)
Async XLA Ops:
  7.2 37.7 %copy-start.3 = (bf16[2,64,1024]{2,1,0:T(8,128)(2,1)S(1)}, bf16[2,64,1024]{2,1,0:T(8,128)(2,1)}, u32[]{:S(2)}) copy-start(bf16[2,64,1024]{2,1,0:T(8,128)(2,1)} %param.15) | copy-start | bytes 786436
  7.2 3.2 copy-start.27
  7.2 15.8 copy-start.28
  7.2 23.6 %copy-start.23 = (bf16[4,256]{1,0:T(4,128)(2,1)S(1)}, bf16[4,256]{1,0:T(4,128)(2,1)}, u32[]{:S(2)}) copy-start(bf16[4,256]{1,0:T(4,128)(2,1)} %param.24) | copy-start | bytes 6148
  7.2 120.7 %all-gather.7.cloned.1.call-start = ((), (), s32[]{:S(2)}) async-start(), calls=%async_computation.9 | async-start | bytes 7864320 | tf_op jit(solution)/shard_map/all_gather | solution.py:116
  8.0 150.9 %all-gather.9.cloned.1.call-start = ((), (), s32[]{:S(2)}) async-start(), calls=%async_computation.10 | async-start | bytes 1310720 | tf_op jit(solution)/shard_map/all_gather | solution.py:141
  10.4 121.2 %copy-start.25 = (f32[128]{0:T(128)}, f32[128]{0:T(128)S(1)}, u32[]{:S(2)}) copy-start(f32[128]{0:T(128)S(1)} %rsqrt.20) | copy-start | bytes 1540
  45.1 86.6 %copy-start.8 = (bf16[128,1024]{1,0:T(8,128)(2,1)}, bf16[128,1024]{1,0:T(8,128)(2,1)S(1)}, u32[]{:S(2)}) copy-start(bf16[128,1024]{1,0:T(8,128)(2,1)S(1)} %add_convert_fusion.1) | copy-start | bytes 786436
  132.5 56.0 %all-gather.11.cloned.1.call-start = ((), (), s32[]{:S(2)}) async-start(), calls=%async_computation.11 | async-start | bytes 1310720 | tf_op jit(solution)/shard_map/all_gather | solution.py:140
  133.3 102.1 %all-gather.13.cloned.1.call-start = ((), (), s32[]{:S(2)}) async-start(), calls=%async_computation.12 | async-start | bytes 2621440 | tf_op jit(solution)/shard_map/all_gather | solution.py:117
  133.9 1.3 copy-start.24
  133.9 14.1 copy-start.11
  133.9 251.2 %all-gather.15.cloned.1.call-start = ((), (), s32[]{:S(2)}) async-start(), calls=%async_computation.13 | async-start | bytes 10485760 | tf_op jit(solution)/shard_map/all_gather | solution.py:118
  134.5 399.9 %all-gather.17.cloned.1.call-start = ((), (), s32[]{:S(2)}) async-start(), calls=%async_computation.14 | async-start | bytes 10485760 | tf_op jit(solution)/shard_map/all_gather | solution.py:119
  135.1 484.2 %reduce-scatter.16.cloned.1.call-start = ((), (), s32[]{:S(2)}) async-start(), calls=%async_computation.15 | async-start | bytes 2621440 | tf_op jit(solution)/shard_map/reduce_scatter | solution.py:192
  147.9 12.4 copy-start.29
  202.3 35.3 %copy-start.10 = (bf16[4,64,512]{2,1,0:T(8,128)(2,1)}, bf16[4,64,512]{2,1,0:T(8,128)(2,1)S(1)}, u32[]{:S(2)}) copy-start(bf16[4,64,512]{2,1,0:T(8,128)(2,1)S(1)} %get-tuple-element.441) | copy-start | bytes 786436
  203.7 190.7 %copy-start.14 = (bf16[16,8,2,512]{3,1,2,0:T(8,128)(2,1)}, bf16[16,8,2,512]{3,1,2,0:T(8,128)(2,1)S(1)}, u32[]{:S(2)}) copy-start(bf16[16,8,2,512]{3,1,2,0:T(8,128)(2,1)S(1)} %copy.78) | copy-start | bytes 786436
  385.1 149.3 %copy-start.17 = (bf16[128,1024]{1,0:T(8,128)(2,1)S(1)}, bf16[128,1024]{1,0:T(8,128)(2,1)}, u32[]{:S(2)}) copy-start(bf16[128,1024]{1,0:T(8,128)(2,1)} %fusion.28) | copy-start | bytes 786436
  534.4 7.3 copy-start.1
  541.7 3.1 copy-start.4
  541.7 3.1 copy-start.12
  541.7 3.3 copy-start.2
  577.2 88.4 %reduce-scatter.18.cloned.1.call-start = ((), (), s32[]{:S(2)}) async-start(), calls=%async_computation.16 | async-start | bytes 2621440 | tf_op jit(solution)/shard_map/reduce_scatter | solution.py:193
  582.9 0.9 copy-start.15
  582.9 161.7 %reduce-scatter.22.cloned.1.call-start = ((), (), s32[]{:S(2)}) async-start(), calls=%async_computation.18 | async-start | bytes 5242880 | tf_op jit(solution)/shard_map/reduce_scatter | solution.py:214
  586.6 1.0 copy-start.16
  586.6 80.1 %copy-start.9 = (bf16[128,1024]{1,0:T(8,128)(2,1)S(1)}, bf16[128,1024]{1,0:T(8,128)(2,1)}, u32[]{:S(2)}) copy-start(bf16[128,1024]{1,0:T(8,128)(2,1)} %copy-done.8) | copy-start | bytes 786436
  586.6 372.7 %reduce-scatter.20.cloned.1.call-start = ((), (), s32[]{:S(2)}) async-start(), calls=%async_computation.17 | async-start | bytes 15728640 | tf_op jit(solution)/shard_map/reduce_scatter | solution.py:213
  587.9 85.1 %copy-start.21 = (bf16[16,8,2,512]{3,1,2,0:T(8,128)(2,1)}, bf16[16,8,2,512]{3,1,2,0:T(8,128)(2,1)S(1)}, u32[]{:S(2)}) copy-start(bf16[16,8,2,512]{3,1,2,0:T(8,128)(2,1)S(1)} %copy.79) | copy-start | bytes 786436
  666.7 6.3 copy-start.20
  673.0 1.5 copy-start.5
  673.0 570.2 %reduce-scatter.24.cloned.1.call-start = ((), (), s32[]{:S(2)}) async-start(), calls=%async_computation.19 | async-start | bytes 20971520 | tf_op jit(solution)/shard_map/reduce_scatter | solution.py:215
  682.7 1.3 copy-start
  682.7 1.3 copy-start.18
  682.7 843.7 %reduce-scatter.26.cloned.1.call-start = ((), (), s32[]{:S(2)}) async-start(), calls=%async_computation.20 | async-start | bytes 20971520 | tf_op jit(solution)/shard_map/reduce_scatter | solution.py:216
  692.1 0.9 copy-start.13
  692.1 1.0 copy-start.30
  692.1 1.4 copy-start.26
  692.2 861.1 %reduce-scatter.28.cloned.1.call-start = ((), (), s32[]{:S(2)}) async-start(), calls=%async_computation.21 | async-start | bytes 655360
  700.0 874.6 %reduce-scatter.30.cloned.1.call-start = ((), (), s32[]{:S(2)}) async-start(), calls=%async_computation.22 | async-start | bytes 655360
  701.3 895.9 %reduce-scatter.32.cloned.1.call-start = ((), (), s32[]{:S(2)}) async-start(), calls=%async_computation.23 | async-start | bytes 655360
  702.5 1071.0 %all-reduce.5.cloned.1.call-start = ((), (), s32[]{:S(2)}) async-start(), calls=%async_computation.24 | async-start | bytes 25165824 | tf_op jit(solution)/shard_map/psum | solution.py:222
  1526.5 0.7 copy-start.31
  1546.8 5.4 copy-start.22
  1552.2 46.1 %dynamic-slice-start = ((f32[4096]{0:T(1024)}, u32[]{:T(128)}), f32[1024]{0:T(1024)S(1)}, s32[]{:S(2)}) async-start(f32[4096]{0:T(1024)} %copy-done.22, u32[]{:T(128)} %multiply.52), calls=%async_computation.25 | async-start | bytes 8704
  1773.5 4.0 copy-start.19
  1773.5 5.0 copy-start.7
  1778.5 3.7 copy-start.6
Sparse Core Ops, SparseCore 0:
  9.6 118.2 all-gather.6
  132.6 26.2 all-gather.8
  161.0 27.4 all-gather.10
  189.9 45.4 all-gather.12
  236.8 148.2 all-gather.14
  386.5 147.8 all-gather.16
  577.3 41.9 reduce-scatter.15
  622.3 43.2 reduce-scatter.17
  668.4 76.1 reduce-scatter.21
  746.9 212.3 reduce-scatter.19
  961.8 281.3 reduce-scatter.23
  1245.4 281.0 reduce-scatter.25
  1529.4 22.3 reduce-scatter.27
  1554.6 19.8 reduce-scatter.29
  1577.3 19.9 reduce-scatter.31
  1601.6 171.8 all-reduce.4
where the time goes:
time: 1790 us
  waiting for transfers between devices  1540 us (86%)
  blocking collectives  88 us (5%)
  matrix products  70.2 us (4%)
  local copies, waits for them, and re-layouts  69.1 us (4%)
    reduce_scatter x1, waiting for transfers between devices, local(): lax.psum_scatter(d_w1, 'shard', scatter_dimension=0, tiled=True)  284 us
    reduce_scatter x1, waiting for transfers between devices, local(): lax.psum_scatter(d_w2, 'shard', scatter_dimension=0, tiled=True)  283 us
    reduce_scatter x1, waiting for transfers between devices, local(): lax.psum_scatter(d_wq, 'shard', scatter_dimension=0, tiled=True)  215 us
    psum x1, waiting for transfers between devices, local(): lax.psum((owned[0], owned[1], owned[2], owned[3], owned[4], owned[5], own...  152 us
    all_gather x1, waiting for transfers between devices, local(): lax.all_gather(w_fc1, 'shard', axis=0, tiled=True)  147 us
    all_gather x1, waiting for transfers between devices, local(): lax.all_gather(w_fc2, 'shard', axis=0, tiled=True)  140 us
    all_gather x1, waiting for transfers between devices, local(): lax.all_gather(w_qkv, 'shard', axis=0, tiled=True)  82.8 us
    reduce_scatter x1, waiting for transfers between devices, local(): lax.psum_scatter(dv_part, 'shard', scatter_dimension=1, tiled=True)  45.2 us
  transfers between devices with their start and end apart: 16, of which 15 were waited for; matrix products, arithmetic and copies ran while one was open for 5% of the time, Pallas kernels for 0%

commit v1 on v0

v1 whole, which is shorter than its diff:
```python
import functools
import math

import jax
import jax.numpy as jnp
from jax import lax
from jax.experimental import pallas as pl
from jax.experimental.pallas import tpu as pltpu
from jax.sharding import PartitionSpec as P

MESH = pl.DeviceIdType.MESH
F32 = jnp.float32
BF16 = jnp.bfloat16
HEAD = 64
PLANE = 8
RANKS = 4
SLOTS = 2
SEMS = 192


def mm(a, b):
    return jnp.dot(a, b, preferred_element_type=F32)


def mm_nt(a, b):
    return lax.dot_general(a, b, (((1,), (1,)), ((), ())), preferred_element_type=F32)


def mm_tn(a, b):
    return lax.dot_general(a, b, (((0,), (0,)), ((), ())), preferred_element_type=F32)


def normed(v):
    centre = v - jnp.mean(v, axis=-1, keepdims=True)
    spread = jnp.mean(centre * centre, axis=-1, keepdims=True)
    inverse = lax.rsqrt(spread + 1e-6)
    return centre * inverse, inverse


def norm_back(e, xh, inverse):
    first = jnp.mean(e, axis=-1, keepdims=True)
    second = jnp.mean(e * xh, axis=-1, keepdims=True)
    return inverse * (e - first - xh * second)


def kernel(
    Z,
    live, clips, cot, smalls, w_qkv, w_out, w_fc1, w_fc2,
    out_k, cg_k, oq, oo, o1, o2, sm_out,
    rc, cm, dmt, smg, tmp, wq, wo, w1, w2,
    n1, n2, dmb, dab, qkv, probs, ob, ab, mb, d2b, d1b, ra, rm, rd2, rd1,
    h1, dh1, slope, gb, dub, dob, dqkv, gq, go, g1, g2,
    cq, co, c1, c2, zq, zo, z1, z2, fq, fo, f1, f2,
    outb, cgb, sms, smc, smz, smx, outr, cgr,
    ssem, rsem, lsem,
):
    replica = lax.axis_index("replica")
    z = lax.axis_index("shard")
    r8 = replica % PLANE
    base = replica - r8
    q = r8 // 2
    c = r8 % 2
    qx = (q // 2) * 2 + (1 - q % 2)
    qy = (1 - q // 2) * 2 + q % 2
    peers = (qx, qy, 3 - q)

    def dev(rank, core, plane):
        return (base + 2 * rank + core, plane)

    partner = dev(q, 1 - c, z)

    sems = iter(range(SEMS))

    def take(n):
        first = next(sems)
        for _ in range(n - 1):
            next(sems)
        return first

    pending = []

    def send(src, dst, sem, device, when=None):
        def go_():
            pltpu.make_async_remote_copy(src, dst, ssem.at[sem], rsem.at[sem], device_id=device, device_id_type=MESH).start()

        def end_():
            pltpu.make_async_remote_copy(src, dst, ssem.at[sem], rsem.at[sem], device_id=device, device_id_type=MESH).wait_send()

        if when is None:
            go_()
            pending.append(end_)
        else:
            pl.when(when)(go_)
            pending.append(lambda: pl.when(when)(end_))

    def arrive(dst, sem, when=None):
        def go_():
            pltpu.make_async_remote_copy(dst, dst, ssem.at[sem], rsem.at[sem], device_id=partner, device_id_type=MESH).wait_recv()

        if when is None:
            go_()
        else:
            pl.when(when)(go_)

    def target(s):
        return (q + z) % RANKS, (q + 2 * s + c) % RANKS

    def origin(s):
        a = (z - 2 * s - c + 2 * RANKS) % RANKS
        return a, (q - a + RANKS) % RANKS

    moves = [target(s) for s in range(SLOTS)]
    backs = [origin(s) for s in range(SLOTS)]

    def stays(place):
        return jnp.logical_and(place[0] == q, place[1] == z)

    barrier = pltpu.get_barrier_semaphore()
    for rank in peers:
        pl.semaphore_signal(barrier, inc=1, device_id=dev(rank, c, z), device_id_type=MESH)
    pl.semaphore_signal(barrier, inc=1, device_id=partner, device_id_type=MESH)
    for d in range(1, Z):
        pl.semaphore_signal(barrier, inc=1, device_id=(replica, (z + d) % Z), device_id_type=MESH)
    count = RANKS - 1 + 1 + Z - 1
    for place in moves + backs:

        @pl.when(jnp.logical_not(stays(place)))
        def _(place=place):
            pl.semaphore_signal(barrier, inc=1, device_id=dev(place[0], c, place[1]), device_id_type=MESH)

        count = count + jnp.where(stays(place), 0, 1)
    pl.semaphore_wait(barrier, count)

    def exchange(src, dst, sem, places):
        for s in range(SLOTS):
            to = dev(places[s][0], c, places[s][1])
            send(src.at[s], dst.at[s], sem + s, to, when=jnp.logical_not(stays(places[s])))

            @pl.when(stays(places[s]))
            def _(s=s):
                pltpu.make_async_copy(src.at[s], dst.at[s], rsem.at[sem + s]).start()

    def exchange_wait(dst, sem):
        for s in range(SLOTS):
            arrive(dst.at[s], sem + s)

    loads = []

    def load(src, dst, k):
        cp = pltpu.make_async_copy(src, dst, lsem.at[k])
        cp.start()
        return cp

    e_clips, e_cot, e_out, e_cg = take(2), take(2), take(2), take(2)
    exchange(clips, rc, e_clips, moves)

    strip = (q // 2) * 128
    loads_q = [
        load(w_qkv.at[:, pl.ds(pl.multiple_of(t * 1024 + zz * 256 + strip, 128), 128)], tmp.at[t * RANKS + zz], t * RANKS + zz)
        for t in range(3)
        for zz in range(RANKS)
    ]
    loads_o = [
        load(w_out.at[pl.ds(pl.multiple_of(q * HEAD, HEAD), HEAD), :], wo.at[z], 12),
    ]
    loads_1 = [
        load(w_fc1.at[:, pl.ds(pl.multiple_of(zz * 1024 + q * 256, 256), 256)], w1.at[z, :, pl.ds(zz * 256, 256)], 13 + zz)
        for zz in range(RANKS)
    ]
    loads_2 = [load(w_fc2.at[pl.ds(pl.multiple_of(q * 256, 256), 256), :], w2.at[z], 17)]

    s_small = take(3)
    smg[z] = smalls[...]
    for d in range(1, Z):
        send(smalls, smg.at[z], s_small + d - 1, (replica, (z + d) % Z))

    for s in range(SLOTS):
        alive = jnp.where(live[0] > s, 1.0, 0.0).astype(F32)
        cm[s] = (cot[s].astype(F32) * alive).astype(BF16)

    def line_step(w, half, sem, i):
        rows = pl.ds(pl.multiple_of(c * half, half), half)
        up = jnp.logical_and(z - i >= 0, z < Z - 1)
        uc = jnp.maximum(z - i, 0)
        send(w.at[uc, rows], w.at[uc, rows], sem + i, (replica, jnp.minimum(z + 1, Z - 1)), when=up)
        down = jnp.logical_and(z + i <= Z - 1, z > 0)
        dc = jnp.minimum(z + i, Z - 1)
        send(w.at[dc, rows], w.at[dc, rows], sem + Z - 1 + i, (replica, jnp.maximum(z - 1, 0)), when=down)

    def line_wait(w, half, sem, i):
        rows = pl.ds(pl.multiple_of(c * half, half), half)
        arrive(w.at[jnp.maximum(z - 1 - i, 0), rows], sem + i, when=z - 1 - i >= 0)
        arrive(w.at[jnp.minimum(z + 1 + i, Z - 1), rows], sem + Z - 1 + i, when=z + 1 + i <= Z - 1)

    def core_share(w, half, sem):
        rows = pl.ds(pl.multiple_of(c * half, half), half)
        for d in range(1, Z):
            zz = (z + d) % Z
            send(w.at[zz, rows], w.at[zz, rows], sem + zz, partner)

    def core_share_wait(w, half, sem):
        rows = pl.ds(pl.multiple_of((1 - c) * half, half), half)
        for d in range(1, Z):
            zz = (z + d) % Z
            arrive(w.at[zz, rows], sem + zz)

    a_q, a_o, a_1, a_2 = (take(2 * (Z - 1)) for _ in range(4))
    k_q, k_o, k_1, k_2 = (take(Z) for _ in range(4))

    for cp in loads_q:
        cp.wait()
    lane = lax.broadcasted_iota(jnp.int32, (256, 128), 1)
    even = q % 2 == 0
    for t in range(3):
        for pair in range(2):
            left = tmp[t * RANKS + 2 * pair].astype(F32)
            right = tmp[t * RANKS + 2 * pair + 1].astype(F32)
            lo = jnp.where(even, left, pltpu.roll(left, HEAD, 1))
            hi = jnp.where(even, pltpu.roll(right, HEAD, 1), right)
            wq[z, :, t * 256 + pair * 128 : t * 256 + pair * 128 + 128] = jnp.where(lane < HEAD, lo, hi).astype(BF16)
    for cp in loads_o:
        cp.wait()
    line_step(wq, 128, a_q, 0)
    line_step(wo, 32, a_o, 0)

    def plane_gather(buf, sem):
        for k, rank in enumerate(peers):
            send(buf.at[:, q], buf.at[:, q], sem + k, dev(rank, c, z))

    def plane_gather_wait(buf, sem):
        for k, rank in enumerate(peers):
            arrive(buf.at[:, rank], sem + k)

    def plane_scatter(buf, dst, sem):
        for k, rank in enumerate(peers):
            send(buf.at[:, rank], dst.at[k], sem + k, dev(rank, c, z))

    def plane_scatter_sum(buf, dst, sem):
        for k in range(RANKS - 1):
            arrive(dst.at[k], sem + k)
        total = buf[:, q].astype(F32)
        for k in range(RANKS - 1):
            total = total + dst[k].astype(F32)
        return total.reshape(SLOTS * 64, 1024)

    for d in range(1, Z):
        arrive(smg.at[(z - d + Z) % Z], s_small + d - 1)

    def row(i):
        return jnp.concatenate([smg[zz, i : i + 1, :] for zz in range(Z)], axis=1)

    exchange_wait(rc, e_clips)
    x = rc[...].astype(F32).reshape(128, 1024)
    xh, _ = normed(x)
    p_n1, p_a, p_n2, p_dm, p_m, p_d2, p_da, p_d1 = (take(3) for _ in range(8))
    n1[:, q] = (xh * row(0) + row(2)).astype(BF16).reshape(SLOTS, 64, 1024)
    plane_gather(n1, p_n1)

    line_wait(wq, 128, a_q, 0)
    line_step(wq, 128, a_q, 1)
    line_wait(wo, 32, a_o, 0)
    line_step(wo, 32, a_o, 1)
    line_wait(wq, 128, a_q, 1)
    line_step(wq, 128, a_q, 2)
    line_wait(wo, 32, a_o, 1)
    line_step(wo, 32, a_o, 2)
    for cp in loads_1 + loads_2:
        cp.wait()
    line_step(w1, 128, a_1, 0)
    line_wait(wq, 128, a_q, 2)
    core_share(wq, 128, k_q)
    line_wait(wo, 32, a_o, 2)
    core_share(wo, 32, k_o)
    plane_gather_wait(n1, p_n1)
    exchange(cm, dmt, e_cot, moves)
    core_share_wait(wq, 128, k_q)

    bias_q = smg[0, 12:13, :] + smg[1, 12:13, :] + smg[2, 12:13, :] + smg[3, 12:13, :]
    bias_v = smg[0, 13:14, :] + smg[1, 13:14, :] + smg[2, 13:14, :] + smg[3, 13:14, :]

    def qkv_step(s, _):
        left = n1[s].reshape(256, 1024)
        for t in range(3):
            val = mm(left, wq[:, :, t * 256 : t * 256 + 256].reshape(1024, 256))
            if t == 0:
                val = val + bias_q
            if t == 2:
                val = val + bias_v
            qkv[t, s] = val.astype(BF16)
        return 0

    lax.fori_loop(0, SLOTS, qkv_step, 0)
    line_wait(w1, 128, a_1, 0)
    line_step(w1, 128, a_1, 1)

    def attend(i, _):
        s = i // 2
        pair = i % 2
        cols = pl.ds(pl.multiple_of(pair * 128, 128), 128)
        qq, kk, vv = qkv[0, s, :, cols], qkv[1, s, :, cols], qkv[2, s, :, cols]
        outs = []
        for j in range(2):
            h = slice(j * HEAD, j * HEAD + HEAD)
            score = mm_nt(qq[:, h], kk[:, h]) * (1.0 / math.sqrt(HEAD))
            e = jnp.exp(score - jnp.max(score, axis=-1, keepdims=True))
            p = e / jnp.sum(e, axis=-1, keepdims=True)
            probs[i, j] = p
            outs.append(mm(p.astype(BF16), vv[:, h]))
        ob[s, :, cols] = jnp.concatenate(outs, axis=1).astype(BF16)
        return 0

    lax.fori_loop(0, 2 * SLOTS, attend, 0)
    core_share_wait(wo, 32, k_o)

    def proj_step(s, _):
        val = mm(ob[s], wo[...].reshape(256, 1024))
        ab[s] = val.astype(BF16).reshape(RANKS, 64, 1024)
        return 0

    lax.fori_loop(0, SLOTS, proj_step, 0)
    plane_scatter(ab, ra, p_a)
    line_wait(w1, 128, a_1, 1)
    line_step(w1, 128, a_1, 2)
    line_step(w2, 128, a_2, 0)
    a = plane_scatter_sum(ab, ra, p_a) + row(6)
    hh = x + a
    h1[...] = hh
    xh2, _ = normed(hh)
    n2[:, q] = (xh2 * row(1) + row(3)).astype(BF16).reshape(SLOTS, 64, 1024)
    plane_gather(n2, p_n2)
    exchange_wait(dmt, e_cot)
    dmb[:, q] = dmt[...]
    plane_gather(dmb, p_dm)
    line_wait(w1, 128, a_1, 2)
    core_share(w1, 128, k_1)
    line_wait(w2, 128, a_2, 0)
    line_step(w2, 128, a_2, 1)
    core_share_wait(w1, 128, k_1)
    plane_gather_wait(n2, p_n2)

    def fc1_step(i, _):
        s = i // RANKS
        zz = i % RANKS
        cols = pl.ds(pl.multiple_of(zz * 256, 256), 256)
        u = mm(n2[s].reshape(256, 1024), w1[:, :, cols].reshape(1024, 256)) + smg[zz, pl.ds(8 + q, 1), :]
        cdf = 0.5 * (1.0 + lax.erf(u * (1.0 / math.sqrt(2.0))))
        gb[s, :, cols] = (u * cdf).astype(BF16)
        slope[s, :, cols] = cdf + u * jnp.exp(-0.5 * u * u) * (1.0 / math.sqrt(2.0 * math.pi))
        return 0

    lax.fori_loop(0, SLOTS * RANKS, fc1_step, 0)
    line_wait(w2, 128, a_2, 1)
    line_step(w2, 128, a_2, 2)
    plane_gather_wait(dmb, p_dm)
    line_wait(w2, 128, a_2, 2)
    core_share(w2, 128, k_2)
    core_share_wait(w2, 128, k_2)

    def du_step(i, _):
        s = i // RANKS
        zz = i % RANKS
        cols = pl.ds(pl.multiple_of(zz * 256, 256), 256)
        dg = mm_nt(dmb[s].reshape(256, 1024), w2[zz])
        dub[s, :, cols] = (dg * slope[s, :, cols]).astype(BF16)
        return 0

    lax.fori_loop(0, SLOTS * RANKS, du_step, 0)

    def dn2_step(i, _):
        s = i // RANKS
        zz = i % RANKS
        cols = pl.ds(pl.multiple_of(zz * 256, 256), 256)
        d2b[s, :, :, cols] = mm_nt(dub[s], w1[zz]).astype(BF16).reshape(RANKS, 64, 256)
        return 0

    lax.fori_loop(0, SLOTS * RANKS, dn2_step, 0)
    plane_scatter(d2b, rd2, p_d2)

    t_core = [take(1) for _ in range(4)]
    t_line = [take(Z - 1) for _ in range(4)]
    t_rank = [take(3) for _ in range(4)]
    t_pass = [take(4) for _ in range(4)]
    halves = (128, 32, 128, 128)
    grads = (gq, go, g1, g2)
    cores = (cq, co, c1, c2)
    lines = (zq, zo, z1, z2)
    finals = (fq, fo, f1, f2)
    results = (oq, oo, o1, o2)

    def reduce_a(w):
        half = halves[w]
        other = pl.ds(pl.multiple_of((1 - c) * half, half), half)
        send(grads[w].at[:, other], cores[w], t_core[w], partner)

    def reduce_b(w):
        half = halves[w]
        mine = pl.ds(pl.multiple_of(c * half, half), half)
        arrive(cores[w], t_core[w])

        def step(zz, _):
            grads[w][zz, mine] = (grads[w][zz, mine].astype(F32) + cores[w][zz].astype(F32)).astype(BF16)
            return 0

        lax.fori_loop(0, Z, step, 0)
        for d in range(1, Z):
            zz = (z + d) % Z
            send(grads[w].at[zz, mine], lines[w].at[d - 1], t_line[w] + d - 1, (replica, zz))

    def reduce_c(w):
        half = halves[w]
        mine = pl.ds(pl.multiple_of(c * half, half), half)
        for d in range(Z - 1):
            arrive(lines[w].at[d], t_line[w] + d)
        total = grads[w][z, mine].astype(F32)
        for d in range(Z - 1):
            total = total + lines[w][d].astype(F32)
        finals[w][...] = total.astype(BF16)
        place = results[w].at[q, mine]
        for k, rank in enumerate(peers):
            send(finals[w], place, t_rank[w] + k, dev(rank, c, z))
        send(finals[w], place, t_pass[w] + 3, partner)
        cp = pltpu.make_async_copy(finals[w], place, lsem.at[18 + w])
        cp.start()
        pending.append(cp.wait)

    def reduce_d(w):
        half = halves[w]
        mine = pl.ds(pl.multiple_of(c * half, half), half)
        for k, rank in enumerate(peers):
            arrive(results[w].at[rank, mine], t_rank[w] + k)
            send(results[w].at[rank, mine], results[w].at[rank, mine], t_pass[w] + k, partner)

    def reduce_e(w):
        half = halves[w]
        theirs = pl.ds(pl.multiple_of((1 - c) * half, half), half)
        for k, rank in enumerate(peers):
            arrive(results[w].at[rank, theirs], t_pass[w] + k)
        arrive(results[w].at[q, theirs], t_pass[w] + 3)

    def dw2_step(zz, _):
        cols = pl.ds(pl.multiple_of(zz * 256, 256), 256)
        left = gb[:, :, cols].reshape(512, 256)
        g2[zz] = mm_tn(left, dmb[...].reshape(512, 1024)).astype(BF16)
        return 0

    lax.fori_loop(0, RANKS, dw2_step, 0)
    reduce_a(3)

    def dw1_step(zz, _):
        cols = pl.ds(pl.multiple_of(zz * 256, 256), 256)
        left = n2[:, :, :, cols].reshape(512, 256)
        g1[zz] = mm_tn(left, dub[...].reshape(512, 1024)).astype(BF16)
        return 0

    lax.fori_loop(0, RANKS, dw1_step, 0)
    reduce_a(2)
    reduce_b(3)

    def m_step(s, _):
        mb[s] = mm(gb[s], w2[...].reshape(1024, 1024)).astype(BF16).reshape(RANKS, 64, 1024)
        return 0

    lax.fori_loop(0, SLOTS, m_step, 0)
    reduce_b(2)

    sms[...] = jnp.zeros((16, 1024), F32)
    fc1_sum = jnp.sum(dub[...].astype(F32).reshape(512, 1024), axis=0, keepdims=True)
    sms[pl.ds(9 + 2 * q, 1), :] = fc1_sum

    def own(i, val):
        sms[i : i + 1, :] = jnp.sum(val, axis=0, keepdims=True)

    dy = dmt[...].astype(F32).reshape(128, 1024)
    own(7, dy)
    dn2 = plane_scatter_sum(d2b, rd2, p_d2)
    xh2, inv2 = normed(h1[...])
    own(1, dn2 * xh2)
    own(3, dn2)
    res = dy + norm_back(dn2 * row(1), xh2, inv2)
    dh1[...] = res
    da = res.astype(BF16)
    dab[:, q] = da.reshape(SLOTS, 64, 1024)
    plane_gather(dab, p_da)
    own(6, da.astype(F32))
    plane_scatter(mb, rm, p_m)
    plane_gather_wait(dab, p_da)

    def do_step(s, _):
        dob[s] = mm_nt(dab[s].reshape(256, 1024), wo[...].reshape(256, 1024)).astype(BF16)
        return 0

    lax.fori_loop(0, SLOTS, do_step, 0)

    def attend_back(i, _):
        s = i // 2
        pair = i % 2
        cols = pl.ds(pl.multiple_of(pair * 128, 128), 128)
        qq, kk, vv, dd = qkv[0, s, :, cols], qkv[1, s, :, cols], qkv[2, s, :, cols], dob[s, :, cols]
        dqs, dks, dvs = [], [], []
        for j in range(2):
            h = slice(j * HEAD, j * HEAD + HEAD)
            p = probs[i, j]
            dp = mm_nt(dd[:, h], vv[:, h])
            ds = (p * (dp - jnp.sum(p * dp, axis=-1, keepdims=True))).astype(BF16)
            dqs.append(mm(ds, kk[:, h]) * (1.0 / math.sqrt(HEAD)))
            dks.append(mm_tn(ds, qq[:, h]) * (1.0 / math.sqrt(HEAD)))
            dvs.append(mm_tn(p.astype(BF16), dd[:, h]))
        dqkv[0, s, :, cols] = jnp.concatenate(dqs, axis=1).astype(BF16)
        dqkv[1, s, :, cols] = jnp.concatenate(dks, axis=1).astype(BF16)
        dqkv[2, s, :, cols] = jnp.concatenate(dvs, axis=1).astype(BF16)
        return 0

    lax.fori_loop(0, 2 * SLOTS, attend_back, 0)

    def dn1_step(i, _):
        s = i // RANKS
        zz = i % RANKS
        cols = pl.ds(pl.multiple_of(zz * 256, 256), 256)
        val = mm_nt(dqkv[0, s], wq[zz, :, 0:256])
        val = val + mm_nt(dqkv[1, s], wq[zz, :, 256:512])
        val = val + mm_nt(dqkv[2, s], wq[zz, :, 512:768])
        d1b[s, :, :, cols] = val.astype(BF16).reshape(RANKS, 64, 256)
        return 0

    lax.fori_loop(0, SLOTS * RANKS, dn1_step, 0)
    plane_scatter(d1b, rd1, p_d1)

    def dwq_step(zz, _):
        cols = pl.ds(pl.multiple_of(zz * 256, 256), 256)
        left = n1[:, :, :, cols].reshape(512, 256)
        for t in range(3):
            gq[zz, :, t * 256 : t * 256 + 256] = mm_tn(left, dqkv[t].reshape(512, 256)).astype(BF16)
        return 0

    lax.fori_loop(0, RANKS, dwq_step, 0)
    reduce_a(0)
    go[...] = mm_tn(ob[...].reshape(512, 256), dab[...].reshape(512, 1024)).astype(BF16).reshape(Z, HEAD, 1024)
    reduce_a(1)
    reduce_b(0)
    reduce_b(1)
    reduce_c(3)
    reduce_c(2)

    m = plane_scatter_sum(mb, rm, p_m) + row(7)
    outb[...] = (h1[...] + m).astype(BF16).reshape(SLOTS, 64, 1024)
    exchange(outb, outr, e_out, backs)

    dq_sum = jnp.sum(dqkv[0].astype(F32).reshape(512, 256), axis=0, keepdims=True)
    dv_sum = jnp.sum(dqkv[2].astype(F32).reshape(512, 256), axis=0, keepdims=True)
    gap = jnp.zeros((1, 128), F32)
    pieces = []
    for zz in range(Z):
        h = slice(zz * HEAD, zz * HEAD + HEAD)
        pieces += [dq_sum[:, h], dv_sum[:, h], gap]
    sms[pl.ds(8 + 2 * q, 1), :] = jnp.concatenate(pieces, axis=1)

    dn1 = plane_scatter_sum(d1b, rd1, p_d1)
    xh, inv = normed(rc[...].astype(F32).reshape(128, 1024))
    own(0, dn1 * xh)
    own(2, dn1)
    cgb[...] = (dh1[...] + norm_back(dn1 * row(0), xh, inv)).astype(BF16).reshape(SLOTS, 64, 1024)
    exchange(cgb, cgr, e_cg, backs)

    u_core, u_line, u_rank = take(1), take(3), take(3)
    send(sms, smc, u_core, partner)
    reduce_c(0)
    reduce_c(1)
    arrive(smc, u_core)
    both = sms[...] + smc[...]
    for zz in range(Z):
        smx[0, zz] = both[:, zz * 256 : zz * 256 + 256]
    for d in range(1, Z):
        send(smx.at[0, (z + d) % Z], smz.at[d - 1], u_line + d - 1, (replica, (z + d) % Z))
    reduce_d(3)
    reduce_d(2)
    for d in range(Z - 1):
        arrive(smz.at[d], u_line + d)
    smx[1, 0] = smx[0, z] + smz[0] + smz[1] + smz[2]
    for k, rank in enumerate(peers):
        send(smx.at[1, 0], smx.at[1, 1 + k], u_rank + k, dev(rank, c, z))
    reduce_d(0)
    reduce_d(1)
    for k in range(RANKS - 1):
        arrive(smx.at[1, 1 + k], u_rank + k)
    sm_out[...] = smx[1, 0] + smx[1, 1] + smx[1, 2] + smx[1, 3]

    exchange_wait(outr, e_out)
    out_k[...] = outr[...]
    exchange_wait(cgr, e_cg)
    cg_k[...] = cgr[...]
    for w in (3, 2, 0, 1):
        reduce_e(w)
    for end in pending:
        end()


def local(
    n_replica,
    Z,
    clips, cotangent, live_count, w_qkv, w_out, w_fc1, w_fc2, norm_gain, norm_bias, proj_bias, fc1_bias,
):
    z = lax.axis_index("shard")
    q = (lax.axis_index("replica") % PLANE) // 2
    spread = lax.dynamic_slice(proj_bias, (0, q * HEAD), (2, HEAD))
    spread = lax.dynamic_update_slice(jnp.zeros((2, 256), BF16), spread, (0, z * HEAD))
    smalls = jnp.concatenate(
        [norm_gain, norm_bias, proj_bias, fc1_bias.reshape(4, 256), spread, jnp.zeros((2, 256), BF16)], axis=0
    ).astype(F32)
    vm = pl.BlockSpec(memory_space=pltpu.VMEM)
    anyspace = pl.BlockSpec(memory_space=pl.ANY)
    shape = jax.ShapeDtypeStruct
    tile = (SLOTS, 64, 1024)
    group = (SLOTS, RANKS, 64, 1024)
    V = pltpu.VMEM
    scratch = [
        V(tile, BF16), V(tile, BF16), V(tile, BF16), V((4, 16, 256), F32), V((12, 256, 128), BF16),
        V((4, 256, 768), BF16), V((4, 64, 1024), BF16), V((4, 256, 1024), BF16), V((4, 256, 1024), BF16),
        V(group, BF16), V(group, BF16), V(group, BF16), V(group, BF16),
        V((3, SLOTS, 256, 256), BF16), V((4, 2, 256, 256), F32), V((SLOTS, 256, 256), BF16),
        V(group, BF16), V(group, BF16), V(group, BF16), V(group, BF16),
        V((3,) + tile, BF16), V((3,) + tile, BF16), V((3,) + tile, BF16), V((3,) + tile, BF16),
        V((128, 1024), F32), V((128, 1024), F32), V((SLOTS, 256, 1024), F32), V((SLOTS, 256, 1024), BF16),
        V((SLOTS, 256, 1024), BF16), V((SLOTS, 256, 256), BF16), V((3, SLOTS, 256, 256), BF16),
        V((4, 256, 768), BF16), V((4, 64, 1024), BF16), V((4, 256, 1024), BF16), V((4, 256, 1024), BF16),
        V((4, 128, 768), BF16), V((4, 32, 1024), BF16), V((4, 128, 1024), BF16), V((4, 128, 1024), BF16),
        V((3, 128, 768), BF16), V((3, 32, 1024), BF16), V((3, 128, 1024), BF16), V((3, 128, 1024), BF16),
        V((128, 768), BF16), V((32, 1024), BF16), V((128, 1024), BF16), V((128, 1024), BF16),
        V(tile, BF16), V(tile, BF16), V((16, 1024), F32), V((16, 1024), F32), V((3, 16, 256), F32), V((2, 4, 16, 256), F32),
        V(tile, BF16), V(tile, BF16),
        pltpu.SemaphoreType.DMA((SEMS,)), pltpu.SemaphoreType.DMA((SEMS,)), pltpu.SemaphoreType.DMA((24,)),
    ]
    out_k, cg_k, oq, oo, o1, o2, sm = pl.pallas_call(
        functools.partial(kernel, Z),
        out_shape=(
            shape(tile, BF16), shape(tile, BF16), shape((4, 256, 768), BF16), shape((4, 64, 1024), BF16),
            shape((4, 256, 1024), BF16), shape((4, 256, 1024), BF16), shape((16, 256), F32),
        ),
        in_specs=[pl.BlockSpec(memory_space=pltpu.SMEM), vm, vm, vm, anyspace, anyspace, anyspace, anyspace],
        out_specs=(vm, vm, anyspace, anyspace, anyspace, anyspace, vm),
        scratch_shapes=scratch,
        compiler_params=pltpu.CompilerParams(
            collective_id=0, has_side_effects=True, vmem_limit_bytes=60 * 2**20
        ),
        cost_estimate=pl.CostEstimate(flops=10**10, bytes_accessed=2**25, transcendentals=2**21),
    )(live_count, clips, cotangent, smalls, w_qkv, w_out, w_fc1, w_fc2)
    alive = (jnp.arange(SLOTS, dtype=jnp.int32) < live_count[0]).astype(BF16)[:, None, None]
    out = out_k * alive
    clips_grad = cg_k.astype(F32)
    d_wq = oq.astype(F32).reshape(4, 256, 3, 4, HEAD).transpose(1, 2, 3, 0, 4).reshape(256, 3072)
    d_wo = oo.astype(F32).reshape(256, 1024)
    d_w1 = o1.astype(F32).reshape(4, 256, 4, 256).transpose(1, 2, 0, 3).reshape(256, 4096)
    d_w2 = o2.astype(F32).reshape(1024, 1024)
    d_q = sm[8::2, 0:HEAD].reshape(1, 256)
    d_v = sm[8::2, HEAD : 2 * HEAD].reshape(1, 256)
    d_gain, d_nbias = sm[0:2], sm[2:4]
    d_pbias = jnp.concatenate([d_q, d_v, sm[6:8]], axis=0)
    d_fbias = sm[9::2].reshape(1024)
    summed = (d_wq, d_wo, d_w1, d_w2, d_gain, d_nbias, d_pbias, d_fbias)
    if n_replica > PLANE:
        groups = [list(range(i, n_replica, PLANE)) for i in range(PLANE)]
        summed = lax.psum(summed, "replica", axis_index_groups=groups)
    return (out, clips_grad) + tuple(summed)


def solution(mesh):
    in_specs = (
        P("replica", "shard", None),
        P("replica", "shard", None),
        P("replica"),
        P("shard", None),
        P("shard", None),
        P("shard", None),
        P("shard", None),
        P(None, "shard"),
        P(None, "shard"),
        P(None, "shard"),
        P("shard"),
    )
    out_specs = (
        P("replica", "shard", None),
        P("replica", "shard", None),
        P("shard", None),
        P("shard", None),
        P("shard", None),
        P("shard", None),
        P(None, "shard"),
        P(None, "shard"),
        P(None, "shard"),
        P("shard"),
    )
    body = functools.partial(local, mesh.shape["replica"], mesh.shape["shard"])
    return jax.shard_map(body, mesh=mesh, in_specs=in_specs, out_specs=out_specs, check_vma=False)
```

time: 1790 us -> 226 us (0.13)
  the two profiles are of different devices: /device:TPU:0 before, /device:TPU:11 now
where the time goes in v1:
time: 226 us
  Pallas kernels  186 us (82%)
  local copies, waits for them, and re-layouts  31.6 us (14%)
  other arithmetic  6.58 us (3%)
    pallas_call x1, Pallas kernels, local(): pl.pallas_call(functools.partial(kernel, Z), out_shape=(shape(tile, BF16)...  186 us
    reshape x3, local copies, waits for them, and re-layouts, local(): o1.astype(F32).reshape(4, 256, 4, 256).transpose(1, 2, 0, 3)  17.6 us

profile of v1, /device:TPU:11, one launch (start us, length us, event | category | flops | bytes accessed | tf_op | source)
XLA Modules:
  0.0 225.6 jit_solution(11996374492219444801)
XLA Ops:
  0.7 0.8 constant_dynamic-slice_fusion
  1.4 0.2 dynamic_update_slice.3
  1.6 0.7 reshape.69
  2.3 0.8 concatenate.6
  3.1 0.6 convert_element_type.17.smalls
  4.4 186.1 %shard_map.186 = (bf16[2,64,1024]{2,1,0:T(8,128)(2,1)}, bf16[2,64,1024]{2,1,0:T(8,128)(2,1)}, bf16[4,256,768]{2,1,0:T(8,128)(2,1)}, bf16[4,64,1024]{2,1,0:T(8,12...) custom-call(s32[1]{0:T(128)} %copy.29.live, bf16[2,64,1024]{2,1,0:T(8,128)(2,1)} %clips.1, ...), custom_call_target="tpu_custom_call" | custom-call | flops 10000000000 | bytes 33554432 | tf_op jit(solution)/shard_map/pallas_call | solution.py:632
  190.4 1.4 fusion
  191.8 0.7 slice.20
  192.5 0.1 reshape.80
  192.6 0.8 slice.21
  193.4 0.1 reshape.81
  193.5 0.6 pad_maximum_fusion
  194.1 5.0 %reshape.96 = f32[4,256,4,256]{3,2,1,0:T(4,128)} reshape(bf16[4,256,1024]{2,1,0:T(8,128)(2,1)} %get-tuple-element.21) | data formatting | bytes 6291456 | tf_op jit(solution)/shard_map/reshape | solution.py:651
  199.0 6.8 %copy.25 = f32[256,4,4,256]{3,2,1,0:T(4,128)} copy(f32[256,4,4,256]{3,1,0,2:T(4,128)} %bitcast.15) | data formatting | bytes 8388608 | tf_op jit(solution)/shard_map/reshape | solution.py:651
  205.9 5.8 %reshape.88 = f32[256,4096]{1,0:T(8,128)} reshape(f32[256,4,4,256]{3,2,1,0:T(4,128)} %copy.25) | data formatting | bytes 8388608 | tf_op jit(solution)/shard_map/reshape | solution.py:651
  211.6 1.7 copy.23
  213.3 1.9 copy.24
  215.2 0.0 copy-start
  215.2 3.7 %copy.26 = f32[256,3072]{1,0:T(8,128)} copy(f32[256,3072]{0,1:T(8,128)} %bitcast.17) | data formatting | bytes 6291456
  218.9 0.0 copy-done
  218.9 0.0 copy-start.1
  218.9 0.0 copy-start.2
  218.9 0.0 copy-start.3
  218.9 2.6 %bitcast_convert_fusion = f32[1024,1024]{1,0:T(8,128)} fusion(bf16[4,256,1024]{2,1,0:T(8,128)(2,1)S(1)} %copy-done), kind=kLoop, calls=%fused_computation | loop fusion | flops 1048576 | bytes 6291456 | tf_op jit(solution)/shard_map/reshape | solution.py:652
  221.5 0.0 copy-done.1
  221.6 1.1 bitcast_convert_fusion.1
  222.7 0.0 copy-done.2
  222.7 0.8 convert_element_type.19
  223.5 0.0 copy-done.3
  223.5 0.8 broadcast_multiply_fusion
  224.3 0.7 slice.23
  225.0 0.6 copy.27
  (3 shorter events, 0.0 us)
Async XLA Ops:
  215.2 3.7 %copy-start = (bf16[4,256,1024]{2,1,0:T(8,128)(2,1)S(1)}, bf16[4,256,1024]{2,1,0:T(8,128)(2,1)}, u32[]{:S(2)}) copy-start(bf16[4,256,1024]{2,1,0:T(8,128)(2,1)} %get-tuple-element.22) | copy-start | bytes 6291460
  218.9 2.6 %copy-start.1 = (bf16[4,64,1024]{2,1,0:T(8,128)(2,1)S(1)}, bf16[4,64,1024]{2,1,0:T(8,128)(2,1)}, u32[]{:S(2)}) copy-start(bf16[4,64,1024]{2,1,0:T(8,128)(2,1)} %get-tuple-element.20) | copy-start | bytes 1572868
  218.9 3.8 %copy-start.2 = (bf16[2,64,1024]{2,1,0:T(8,128)(2,1)S(1)}, bf16[2,64,1024]{2,1,0:T(8,128)(2,1)}, u32[]{:S(2)}) copy-start(bf16[2,64,1024]{2,1,0:T(8,128)(2,1)} %get-tuple-element.18) | copy-start | bytes 786436
  218.9 4.6 %copy-start.3 = (bf16[2,64,1024]{2,1,0:T(8,128)(2,1)S(1)}, bf16[2,64,1024]{2,1,0:T(8,128)(2,1)}, u32[]{:S(2)}) copy-start(bf16[2,64,1024]{2,1,0:T(8,128)(2,1)} %get-tuple-element.17) | copy-start | bytes 786436

commit v2 on v1

v2 whole, which is shorter than its diff:
```python
import functools
import math

import jax
import jax.numpy as jnp
from jax import lax
from jax.experimental import pallas as pl
from jax.experimental.pallas import tpu as pltpu
from jax.sharding import PartitionSpec as P

MESH = pl.DeviceIdType.MESH
F32 = jnp.float32
BF16 = jnp.bfloat16
HEAD = 64
PLANE = 8
RANKS = 4
SLOTS = 2
SEMS = 198
LOADS = 18
SCALE = 1.0 / math.sqrt(HEAD)


def mm(a, b):
    return jnp.dot(a, b, preferred_element_type=F32)


def mm_nt(a, b):
    return lax.dot_general(a, b, (((1,), (1,)), ((), ())), preferred_element_type=F32)


def mm_tn(a, b):
    return lax.dot_general(a, b, (((0,), (0,)), ((), ())), preferred_element_type=F32)


def normed(v):
    centre = v - jnp.mean(v, axis=-1, keepdims=True)
    spread = jnp.mean(centre * centre, axis=-1, keepdims=True)
    inverse = lax.rsqrt(spread + 1e-6)
    return centre * inverse, inverse


def norm_back(e, xh, inverse):
    first = jnp.mean(e, axis=-1, keepdims=True)
    second = jnp.mean(e * xh, axis=-1, keepdims=True)
    return inverse * (e - first - xh * second)


def strip(i, width=256):
    return pl.ds(pl.multiple_of(i * width, width), width)


def kernel(
    clips, cot, live, gains, nbias, pbias, fbias, w_qkv, w_out, w_fc1, w_fc2,
    out_k, cg_k, oq, oo, o1, o2, sm_out,
    rc, cm, dmt, sml, smg, tmp, wq, wo, w1, w2,
    n1, n2, dmb, dab, qkv, probs, ob, ab, mb, d2b, d1b, ra, rm, rd2, rd1,
    h1, dh1, slope, gb, dub, dob, dqkv, gq, go, g1, g2,
    cq, co, c1, c2, zq, zo, z1, z2, fq, fo, f1, f2,
    outb, cgb, sms, smc, smz, smx, outr, cgr,
    ssem, rsem, lsem,
):
    Z = 4
    replica = lax.axis_index("replica")
    z = lax.axis_index("shard")
    r8 = replica % PLANE
    base = replica - r8
    q = r8 // 2
    c = r8 % 2
    qx = (q // 2) * 2 + (1 - q % 2)
    qy = (1 - q // 2) * 2 + q % 2
    qd = 3 - q
    lower = z // 2
    mate = 2 * lower + 1 - z % 2
    far_middle = 2 - lower
    far = 2 * (1 - lower)
    middle = jnp.logical_or(z == 1, z == 2)
    end = jnp.logical_not(middle)

    def dev(rank, core, plane):
        return (base + 2 * rank + core, plane)

    px, py, partner = dev(qx, c, z), dev(qy, c, z), dev(q, 1 - c, z)

    counter = [0]

    def take(n):
        counter[0] += n
        return counter[0] - n

    pending = []

    def send(src, dst, sem, device, when=None, out=None, got=None):
        done = sem if out is None else out

        def copy():
            return pltpu.make_async_remote_copy(
                src, dst, ssem.at[done], rsem.at[sem], device_id=device, device_id_type=MESH
            )

        if when is None:
            copy().start()
            pending.append(lambda: copy().wait_send())
        else:
            pl.when(when)(lambda: copy().start())
            pending.append(lambda: pl.when(when)(lambda: copy().wait_send()))

    def arrive(dst, sem):
        pltpu.make_async_remote_copy(
            dst, dst, ssem.at[sem], rsem.at[sem], device_id=partner, device_id_type=MESH
        ).wait_recv()

    def target(s):
        return (q + z) % RANKS, (q + 2 * s + c) % RANKS

    def origin(s):
        a = (z - 2 * s - c + 2 * RANKS) % RANKS
        return a, (q - a + RANKS) % RANKS

    moves = [target(s) for s in range(SLOTS)]
    backs = [origin(s) for s in range(SLOTS)]

    def stays(place):
        return jnp.logical_and(place[0] == q, place[1] == z)

    loads = []

    def load(src, dst):
        cp = pltpu.make_async_copy(src, dst, lsem.at[len(loads)])
        cp.start()
        loads.append(cp)

    pair = (q // 2) * 128
    for t in range(3):
        for zz in range(RANKS):
            load(w_qkv.at[:, pl.ds(pl.multiple_of(t * 1024 + zz * 256 + pair, 128), 128)], tmp.at[t * RANKS + zz])
    load(w_out.at[strip(q, HEAD), :], wo.at[z])

    barrier = pltpu.get_barrier_semaphore()
    for device in (px, py, dev(qd, c, z), partner):
        pl.semaphore_signal(barrier, inc=1, device_id=device, device_id_type=MESH)
    for d in range(1, Z):
        pl.semaphore_signal(barrier, inc=1, device_id=(replica, (z + d) % Z), device_id_type=MESH)
    count = 4 + Z - 1
    for place in moves + backs:

        @pl.when(jnp.logical_not(stays(place)))
        def _(place=place):
            pl.semaphore_signal(barrier, inc=1, device_id=dev(place[0], c, place[1]), device_id_type=MESH)

        count = count + jnp.where(stays(place), 0, 1)

    sml[...] = jnp.zeros((16, 256), F32)
    sml[0:2] = gains[...].astype(F32)
    sml[2:4] = nbias[...].astype(F32)
    sml[4:8] = pbias[...].astype(F32)
    for k in range(RANKS):
        sml[8 + k : 9 + k] = fbias[pl.ds(k * 256, 256)].astype(F32).reshape(1, 256)
    lane = lax.broadcasted_iota(jnp.int32, (8, 256), 1)
    turned = pltpu.roll(sml[0:8], (z * HEAD - q * HEAD + 256) % 256, 1)
    kept = jnp.where(jnp.logical_and(lane >= z * HEAD, lane < z * HEAD + HEAD), turned, 0.0)
    sml[12:14] = kept[4:6]

    pl.semaphore_wait(barrier, count)

    def exchange(src, dst, sem, places):
        for s in range(SLOTS):
            to = dev(places[s][0], c, places[s][1])
            send(src.at[s], dst.at[s], sem + s, to, when=jnp.logical_not(stays(places[s])))

            @pl.when(stays(places[s]))
            def _(s=s):
                pltpu.make_async_copy(src.at[s], dst.at[s], rsem.at[sem + s]).start()

    def exchange_wait(dst, sem):
        for s in range(SLOTS):
            arrive(dst.at[s], sem + s)

    e_clips, e_cot, e_out, e_cg = take(2), take(2), take(2), take(2)
    exchange(clips, rc, e_clips, moves)
    s_small = take(3)
    smg[z] = sml[...]
    for d in range(1, Z):
        send(sml, smg.at[z], s_small + d - 1, (replica, (z + d) % Z))
    n_first = len(loads)
    for zz in range(RANKS):
        load(w_fc1.at[:, pl.ds(pl.multiple_of(zz * 1024 + q * 256, 256), 256)], w1.at[z, :, pl.ds(zz * 256, 256)])
    load(w_fc2.at[strip(q), :], w2.at[z])

    def mine(half):
        return pl.ds(pl.multiple_of(c * half, half), half)

    def theirs(half):
        return pl.ds(pl.multiple_of((1 - c) * half, half), half)

    def line_a(w, half, sem):
        own_part = w.at[z, mine(half)]
        send(own_part, own_part, sem, (replica, mate))
        send(own_part, own_part, sem + 1 + z % 2, (replica, far_middle), got=middle)

    def share(w, half, sem, zz, when=None):
        part = w.at[zz, mine(half)]
        send(part, part, sem + 4 + (zz - z + Z) % Z, partner, when=when)

    def line_b(w, half, sem):
        for f in (lower, 1 - lower):

            @pl.when(middle)
            def _(f=f):
                arrive(w.at[far + f, mine(half)], sem + 1 + f)

            part = w.at[far + f, mine(half)]
            send(part, part, sem + 1 + f, (replica, mate), when=middle, out=sem + 3 + f, got=end)
            share(w, half, sem, far + f, when=middle)

    def line_c(w, half, sem):
        arrive(w.at[mate, mine(half)], sem)
        share(w, half, sem, mate)
        for f in (lower, 1 - lower):

            @pl.when(end)
            def _(f=f):
                arrive(w.at[far + f, mine(half)], sem + 1 + f)

            share(w, half, sem, far + f, when=end)

    def line_d(w, half, sem):
        for zz in (mate, far + lower, far + 1 - lower):
            arrive(w.at[zz, theirs(half)], sem + 4 + (zz - z + Z) % Z)

    a_q, a_o, a_1, a_2 = (take(8) for _ in range(4))

    CUT = 2
    ROWS = 64 // CUT

    def gather_a(buf, sem):
        for j in range(CUT):
            rows = pl.ds(j * ROWS, ROWS)
            send(buf.at[0, q, rows], buf.at[0, q, rows], sem + j, px)
            send(buf.at[1, q, rows], buf.at[1, q, rows], sem + CUT + j, py)
        send(buf.at[1, q], buf.at[1, q], sem + 2 * CUT, px)
        send(buf.at[0, q], buf.at[0, q], sem + 2 * CUT + 1, py)

    def gather_b(buf, sem):
        for j in range(CUT):
            rows = pl.ds(j * ROWS, ROWS)
            arrive(buf.at[0, qx, rows], sem + j)
            send(buf.at[0, qx, rows], buf.at[0, qx, rows], sem + 2 * CUT + 2 + j, py)
            arrive(buf.at[1, qy, rows], sem + CUT + j)
            send(buf.at[1, qy, rows], buf.at[1, qy, rows], sem + 3 * CUT + 2 + j, px)

    def gather_c(buf, sem):
        arrive(buf.at[1, qx], sem + 2 * CUT)
        arrive(buf.at[0, qy], sem + 2 * CUT + 1)
        for j in range(CUT):
            rows = pl.ds(j * ROWS, ROWS)
            arrive(buf.at[0, qd, rows], sem + 2 * CUT + 2 + j)
            arrive(buf.at[1, qd, rows], sem + 3 * CUT + 2 + j)

    def scatter_a(buf, rb, sem):
        send(buf.at[0, qd], rb.at[0], sem, px)
        send(buf.at[1, qd], rb.at[1], sem + 1, py)
        send(buf.at[0, qx], rb.at[2], sem + 2, px)
        send(buf.at[1, qy], rb.at[3], sem + 3, py)

    def scatter_b(buf, rb, sem):
        arrive(rb.at[0], sem)
        rb[6] = (buf[0, qy].astype(F32) + rb[0].astype(F32)).astype(BF16)
        send(rb.at[6], rb.at[4], sem + 4, py)
        arrive(rb.at[1], sem + 1)
        rb[7] = (buf[1, qx].astype(F32) + rb[1].astype(F32)).astype(BF16)
        send(rb.at[7], rb.at[5], sem + 5, px)

    def scatter_c(buf, rb, sem):
        for k in range(2, 6):
            arrive(rb.at[k], sem + k)
        first = buf[0, q].astype(F32) + rb[2].astype(F32) + rb[4].astype(F32)
        second = buf[1, q].astype(F32) + rb[3].astype(F32) + rb[5].astype(F32)
        return jnp.concatenate([first, second], axis=0)

    p_n1, p_n2, p_dm, p_da = (take(4 * CUT + 2) for _ in range(4))
    p_a, p_m, p_d2, p_d1 = (take(6) for _ in range(4))

    WAYS = 6
    t_core = [take(1) for _ in range(WAYS)]
    t_line = [take(6) for _ in range(WAYS)]
    t_rank = [take(6) for _ in range(WAYS)]
    t_pass = [take(1) for _ in range(WAYS)]
    stored = [None] * WAYS
    halves = (128, 32, 128, 128, 128, 128)
    grads = (gq.at[0], go, g1, g2, gq.at[1], gq.at[2])
    cores = (cq.at[0], co, c1, c2, cq.at[1], cq.at[2])
    lines = (zq.at[0], zo, z1, z2, zq.at[1], zq.at[2])
    finals = (fq.at[0], fo, f1, f2, fq.at[1], fq.at[2])
    results = (oq.at[0], oo, o1, o2, oq.at[1], oq.at[2])

    def reduce_a(w):
        send(grads[w].at[:, theirs(halves[w])], cores[w], t_core[w], partner)

    def reduce_b(w):
        rows = mine(halves[w])
        arrive(cores[w], t_core[w])

        def step(zz, _):
            grads[w][zz, rows] = (grads[w][zz, rows].astype(F32) + cores[w][zz].astype(F32)).astype(BF16)
            return 0

        lax.fori_loop(0, Z, step, 0)
        for f in range(2):
            send(grads[w].at[far + f, rows], lines[w].at[2 + f], t_line[w] + 2 + f, (replica, mate), when=end, got=middle)
        send(grads[w].at[mate, rows], lines[w].at[0], t_line[w], (replica, mate))

    def reduce_m(w):
        rows = mine(halves[w])
        for f in range(2):

            @pl.when(middle)
            def _(f=f):
                arrive(lines[w].at[2 + f], t_line[w] + 2 + f)
                grads[w][far + f, rows] = (grads[w][far + f, rows].astype(F32) + lines[w][2 + f].astype(F32)).astype(BF16)

            send(grads[w].at[far + f, rows], lines[w].at[1], t_line[w] + 1, (replica, far + f), when=middle, out=t_line[w] + 4 + f)

    def spots(w, rank, core):
        half = halves[w]
        first = pl.multiple_of(core * half, half)
        second = pl.multiple_of(core * half + half // 2, half // 2)
        return (
            results[w].at[rank, pl.ds(first, half // 2)],
            results[w].at[rank, pl.ds(second, half // 2)],
            results[w].at[rank, pl.ds(first, half)],
        )

    def reduce_c(w):
        half = halves[w]
        for k in range(2):
            arrive(lines[w].at[k], t_line[w] + k)
        total = grads[w][z, mine(half)].astype(F32)
        for k in range(2):
            total = total + lines[w][k].astype(F32)
        finals[w][...] = total.astype(BF16)
        one, two, both = spots(w, q, c)
        a, b = finals[w].at[pl.ds(0, half // 2)], finals[w].at[pl.ds(half // 2, half // 2)]
        send(a, one, t_rank[w], px)
        send(b, two, t_rank[w] + 1, py)
        send(b, two, t_rank[w] + 2, px)
        send(a, one, t_rank[w] + 3, py)
        stored[w] = pltpu.make_async_copy(finals[w], both, lsem.at[LOADS + w])
        stored[w].start()

    def reduce_d(w):
        one = spots(w, qx, c)[0]
        arrive(one, t_rank[w])
        send(one, one, t_rank[w] + 4, py)
        two = spots(w, qy, c)[1]
        arrive(two, t_rank[w] + 1)
        send(two, two, t_rank[w] + 5, px)

    def reduce_e(w):
        arrive(spots(w, qx, c)[1], t_rank[w] + 2)
        arrive(spots(w, qy, c)[0], t_rank[w] + 3)
        arrive(spots(w, qd, c)[0], t_rank[w] + 4)
        arrive(spots(w, qd, c)[1], t_rank[w] + 5)
        stored[w].wait()
        part = results[w].at[:, mine(halves[w])]
        send(part, part, t_pass[w], partner)

    def reduce_f(w):
        arrive(results[w].at[:, theirs(halves[w])], t_pass[w])

    for cp in loads[:n_first]:
        cp.wait()
    lane = lax.broadcasted_iota(jnp.int32, (256, 128), 1)
    even = q % 2 == 0
    for t in range(3):
        for m in range(2):
            left = tmp[t * RANKS + 2 * m].astype(F32)
            right = tmp[t * RANKS + 2 * m + 1].astype(F32)
            lo = jnp.where(even, left, pltpu.roll(left, HEAD, 1))
            hi = jnp.where(even, pltpu.roll(right, HEAD, 1), right)
            wq[z, :, t * 256 + m * 128 : t * 256 + m * 128 + 128] = jnp.where(lane < HEAD, lo, hi).astype(BF16)
    line_a(wq, 128, a_q)

    for s in range(SLOTS):
        alive = jnp.where(live[0] > s, 1.0, 0.0).astype(F32)
        cm[s] = (cot[s].astype(F32) * alive).astype(BF16)

    for d in range(1, Z):
        arrive(smg.at[(z - d + Z) % Z], s_small + d - 1)

    def row(i):
        return jnp.concatenate([smg[zz, i : i + 1, :] for zz in range(Z)], axis=1)

    bias_q = smg[0, 12:13, :] + smg[1, 12:13, :] + smg[2, 12:13, :] + smg[3, 12:13, :]
    bias_v = smg[0, 13:14, :] + smg[1, 13:14, :] + smg[2, 13:14, :] + smg[3, 13:14, :]

    exchange_wait(rc, e_clips)
    x = rc[...].astype(F32).reshape(128, 1024)
    xh, _ = normed(x)
    n1[:, q] = (xh * row(0) + row(2)).astype(BF16).reshape(SLOTS, 64, 1024)
    gather_a(n1, p_n1)
    gather_b(n1, p_n1)
    line_b(wq, 128, a_q)
    line_a(wo, 32, a_o)
    exchange(cm, dmt, e_cot, moves)
    gather_c(n1, p_n1)
    line_c(wq, 128, a_q)
    line_b(wo, 32, a_o)
    for cp in loads[n_first:]:
        cp.wait()
    line_a(w1, 128, a_1)
    line_d(wq, 128, a_q)

    def qkv_step(t, _):
        bias = jnp.where(t == 0, bias_q, jnp.where(t == 2, bias_v, 0.0))
        val = mm(n1[...].reshape(512, 1024), wq[:, :, strip(t)].reshape(1024, 256)) + bias
        qkv[t] = val.astype(BF16).reshape(SLOTS, 256, 256)
        return 0

    lax.fori_loop(0, 3, qkv_step, 0)
    line_c(wo, 32, a_o)
    exchange_wait(dmt, e_cot)
    dmb[:, q] = dmt[...]
    gather_a(dmb, p_dm)

    def attend(i, _):
        s = i // 2
        cols = strip(i % 2, 128)
        qq, kk, vv = qkv[0, s, :, cols], qkv[1, s, :, cols], qkv[2, s, :, cols]
        outs = []
        for j in range(2):
            h = slice(j * HEAD, j * HEAD + HEAD)
            score = mm_nt(qq[:, h], kk[:, h]) * SCALE
            e = jnp.exp(score - jnp.max(score, axis=-1, keepdims=True))
            p = e / jnp.sum(e, axis=-1, keepdims=True)
            probs[i, j] = p
            outs.append(mm(p.astype(BF16), vv[:, h]))
        ob[s, :, cols] = jnp.concatenate(outs, axis=1).astype(BF16)
        return 0

    lax.fori_loop(0, 2 * SLOTS, attend, 0)
    line_d(wo, 32, a_o)

    def proj_step(s, _):
        val = mm(ob[s], wo[...].reshape(256, 1024))
        ab[s] = val.astype(BF16).reshape(RANKS, 64, 1024)
        return 0

    lax.fori_loop(0, SLOTS, proj_step, 0)
    scatter_a(ab, ra, p_a)
    gather_b(dmb, p_dm)
    scatter_b(ab, ra, p_a)
    line_b(w1, 128, a_1)
    line_a(w2, 128, a_2)
    a = scatter_c(ab, ra, p_a) + row(6)
    hh = x + a
    h1[...] = hh
    xh2, _ = normed(hh)
    n2[:, q] = (xh2 * row(1) + row(3)).astype(BF16).reshape(SLOTS, 64, 1024)
    gather_a(n2, p_n2)
    gather_b(n2, p_n2)
    line_c(w1, 128, a_1)
    line_b(w2, 128, a_2)
    line_d(w1, 128, a_1)
    gather_c(n2, p_n2)

    def fc1_step(i, _):
        s = i // RANKS
        zz = i % RANKS
        cols = strip(zz)
        u = mm(n2[s].reshape(256, 1024), w1[:, :, cols].reshape(1024, 256)) + smg[zz, pl.ds(8 + q, 1), :]
        cdf = 0.5 * (1.0 + lax.erf(u * (1.0 / math.sqrt(2.0))))
        gb[s, :, cols] = (u * cdf).astype(BF16)
        slope[s, :, cols] = cdf + u * jnp.exp(-0.5 * u * u) * (1.0 / math.sqrt(2.0 * math.pi))
        return 0

    lax.fori_loop(0, SLOTS * RANKS, fc1_step, 0)
    gather_c(dmb, p_dm)

    def dw2_step(zz, _):
        g2[zz] = mm_tn(gb[:, :, strip(zz)].reshape(512, 256), dmb[...].reshape(512, 1024)).astype(BF16)
        return 0

    lax.fori_loop(0, RANKS, dw2_step, 0)
    reduce_a(3)
    line_c(w2, 128, a_2)
    reduce_b(3)
    line_d(w2, 128, a_2)

    def du_step(zz, _):
        cols = strip(zz)
        dg = mm_nt(dmb[...].reshape(512, 1024), w2[zz]).reshape(SLOTS, 256, 256)
        dub[:, :, cols] = (dg * slope[:, :, cols]).astype(BF16)
        return 0

    lax.fori_loop(0, RANKS, du_step, 0)

    def dn2_step(zz, _):
        val = mm_nt(dub[...].reshape(512, 1024), w1[zz])
        d2b[:, :, :, strip(zz)] = val.astype(BF16).reshape(SLOTS, RANKS, 64, 256)
        return 0

    lax.fori_loop(0, RANKS, dn2_step, 0)
    scatter_a(d2b, rd2, p_d2)

    def dw1_step(zz, _):
        g1[zz] = mm_tn(n2[:, :, :, strip(zz)].reshape(512, 256), dub[...].reshape(512, 1024)).astype(BF16)
        return 0

    lax.fori_loop(0, RANKS, dw1_step, 0)
    reduce_a(2)
    scatter_b(d2b, rd2, p_d2)
    reduce_b(2)

    sms[...] = jnp.zeros((16, 1024), F32)

    def own(i, val):
        sms[i : i + 1, :] = jnp.sum(val, axis=0, keepdims=True)

    dy = dmt[...].astype(F32).reshape(128, 1024)
    own(7, dy)
    xh2, inv2 = normed(h1[...])
    dn2 = scatter_c(d2b, rd2, p_d2)
    res = dy + norm_back(dn2 * row(1), xh2, inv2)
    da = res.astype(BF16)
    dab[:, q] = da.reshape(SLOTS, 64, 1024)
    gather_a(dab, p_da)
    reduce_m(3)
    dh1[...] = res
    own(1, dn2 * xh2)
    own(3, dn2)
    own(6, da.astype(F32))
    fc1_sum = jnp.sum(dub[...].astype(F32).reshape(512, 1024), axis=0, keepdims=True)
    sms[pl.ds(9 + 2 * q, 1), :] = fc1_sum

    def m_step(s, _):
        mb[s] = mm(gb[s], w2[...].reshape(1024, 1024)).astype(BF16).reshape(RANKS, 64, 1024)
        return 0

    lax.fori_loop(0, SLOTS, m_step, 0)
    gather_b(dab, p_da)
    scatter_a(mb, rm, p_m)
    gather_c(dab, p_da)
    go[...] = mm_tn(ob[...].reshape(512, 256), dab[...].reshape(512, 1024)).astype(BF16).reshape(Z, HEAD, 1024)
    reduce_a(1)

    def do_step(s, _):
        dob[s] = mm_nt(dab[s].reshape(256, 1024), wo[...].reshape(256, 1024)).astype(BF16)
        return 0

    lax.fori_loop(0, SLOTS, do_step, 0)
    reduce_b(1)

    def attend_back(i, _):
        s = i // 2
        cols = strip(i % 2, 128)
        qq, kk, vv, dd = qkv[0, s, :, cols], qkv[1, s, :, cols], qkv[2, s, :, cols], dob[s, :, cols]
        dqs, dks, dvs = [], [], []
        for j in range(2):
            h = slice(j * HEAD, j * HEAD + HEAD)
            p = probs[i, j]
            dp = mm_nt(dd[:, h], vv[:, h])
            ds = (p * (dp - jnp.sum(p * dp, axis=-1, keepdims=True))).astype(BF16)
            dqs.append(mm(ds, kk[:, h]) * SCALE)
            dks.append(mm_tn(ds, qq[:, h]) * SCALE)
            dvs.append(mm_tn(p.astype(BF16), dd[:, h]))
        dqkv[0, s, :, cols] = jnp.concatenate(dqs, axis=1).astype(BF16)
        dqkv[1, s, :, cols] = jnp.concatenate(dks, axis=1).astype(BF16)
        dqkv[2, s, :, cols] = jnp.concatenate(dvs, axis=1).astype(BF16)
        return 0

    lax.fori_loop(0, SLOTS, attend_back, 0)
    scatter_b(mb, rm, p_m)
    reduce_c(3)
    lax.fori_loop(SLOTS, 2 * SLOTS, attend_back, 0)
    reduce_m(2)

    def dwq_step(zz, _):
        left = n1[:, :, :, strip(zz)].reshape(512, 256)
        for t in range(3):
            gq[t, zz] = mm_tn(left, dqkv[t].reshape(512, 256)).astype(BF16)
        return 0

    lax.fori_loop(0, RANKS, dwq_step, 0)
    for w in (0, 4, 5):
        reduce_a(w)

    def dn1_step(zz, _):
        val = mm_nt(dqkv[0].reshape(512, 256), wq[zz, :, 0:256])
        val = val + mm_nt(dqkv[1].reshape(512, 256), wq[zz, :, 256:512])
        val = val + mm_nt(dqkv[2].reshape(512, 256), wq[zz, :, 512:768])
        d1b[:, :, :, strip(zz)] = val.astype(BF16).reshape(SLOTS, RANKS, 64, 256)
        return 0

    lax.fori_loop(0, RANKS, dn1_step, 0)
    scatter_a(d1b, rd1, p_d1)
    for w in (0, 4, 5):
        reduce_b(w)
    reduce_d(3)
    m = scatter_c(mb, rm, p_m) + row(7)
    outb[...] = (h1[...] + m).astype(BF16).reshape(SLOTS, 64, 1024)
    exchange(outb, outr, e_out, backs)
    scatter_b(d1b, rd1, p_d1)

    dq_sum = jnp.sum(dqkv[0].astype(F32).reshape(512, 256), axis=0, keepdims=True)
    dv_sum = jnp.sum(dqkv[2].astype(F32).reshape(512, 256), axis=0, keepdims=True)
    gap = jnp.zeros((1, 128), F32)
    pieces = []
    for zz in range(Z):
        h = slice(zz * HEAD, zz * HEAD + HEAD)
        pieces += [dq_sum[:, h], dv_sum[:, h], gap]
    sms[pl.ds(8 + 2 * q, 1), :] = jnp.concatenate(pieces, axis=1)
    xh, inv = normed(rc[...].astype(F32).reshape(128, 1024))
    reduce_m(1)
    reduce_m(0)
    reduce_m(4)
    reduce_c(2)

    dn1 = scatter_c(d1b, rd1, p_d1)
    own(0, dn1 * xh)
    own(2, dn1)
    u_core, u_line, u_rank = take(1), take(3), take(3)
    send(sms, smc, u_core, partner)
    cgb[...] = (dh1[...] + norm_back(dn1 * row(0), xh, inv)).astype(BF16).reshape(SLOTS, 64, 1024)
    exchange(cgb, cgr, e_cg, backs)

    arrive(smc, u_core)
    both = sms[...] + smc[...]
    for zz in range(Z):
        smx[0, zz] = both[:, zz * 256 : zz * 256 + 256]
    for d in range(1, Z):
        send(smx.at[0, (z + d) % Z], smz.at[d - 1], u_line + d - 1, (replica, (z + d) % Z))
    reduce_m(5)
    reduce_c(1)
    reduce_c(0)
    reduce_d(2)
    reduce_e(3)
    reduce_c(4)
    reduce_c(5)
    reduce_e(2)
    for d in range(Z - 1):
        arrive(smz.at[d], u_line + d)
    smx[1, 0] = smx[0, z] + smz[0] + smz[1] + smz[2]
    for k, rank in enumerate((qx, qy, qd)):
        send(smx.at[1, 0], smx.at[1, 1 + k], u_rank + k, dev(rank, c, z))
    for w in (1, 0, 4, 5):
        reduce_d(w)
    for w in (1, 0, 4, 5):
        reduce_e(w)
    for k in range(RANKS - 1):
        arrive(smx.at[1, 1 + k], u_rank + k)
    sm_out[...] = smx[1, 0] + smx[1, 1] + smx[1, 2] + smx[1, 3]

    exchange_wait(outr, e_out)
    out_k[...] = outr[...].reshape(128, 1024)
    exchange_wait(cgr, e_cg)
    cg_k[...] = cgr[...].reshape(128, 1024)
    for w in (3, 2, 1, 0, 4, 5):
        reduce_f(w)
    assert counter[0] <= SEMS, counter[0]
    for finish in pending:
        finish()


def finish_kernel(
    live, out_k, cg_k, oq, oo, o1, o2, sm,
    out, cg, dwq, dwo, dw1, dw2, dgain, dnbias, dpbias, dfbias,
    b_out, b_cg, bq, bo, b1, b2, f_out, f_cg, fq, fo, f1, f2, isem, osem,
):
    ins, outs = [], []

    def fetch(src, dst):
        cp = pltpu.make_async_copy(src, dst, isem.at[len(ins)])
        cp.start()
        ins.append(cp)

    def store(src, dst):
        cp = pltpu.make_async_copy(src, dst, osem.at[len(outs)])
        cp.start()
        outs.append(cp)

    for h in range(2):
        fetch(o2.at[pl.ds(2 * h, 2)], b2.at[pl.ds(2 * h, 2)])
    for h in range(2):
        fetch(o1.at[:, pl.ds(128 * h, 128)], b1.at[:, pl.ds(128 * h, 128)])
    for h in range(2):
        fetch(oq.at[:, :, pl.ds(128 * h, 128)], bq.at[:, :, pl.ds(128 * h, 128)])
    fetch(oo, bo)
    fetch(cg_k, b_cg)
    fetch(out_k, b_out)

    dgain[...] = sm[0:2]
    dnbias[...] = sm[2:4]
    lane = lax.broadcasted_iota(jnp.int32, (1, 128), 1)
    rows = [sm[8 + 2 * k : 9 + 2 * k, 0:128] for k in range(RANKS)]
    turn = [pltpu.roll(r, HEAD, 1) for r in rows]
    for g in range(2):
        a, b = 2 * g, 2 * g + 1
        dpbias[0:1, g * 128 : g * 128 + 128] = jnp.where(lane < HEAD, rows[a], turn[b])
        dpbias[1:2, g * 128 : g * 128 + 128] = jnp.where(lane < HEAD, turn[a], rows[b])
    dpbias[2:4] = sm[6:8]
    for k in range(RANKS):
        dfbias[pl.ds(k * 256, 256)] = sm[9 + 2 * k : 10 + 2 * k, :].reshape(256)

    for h in range(2):
        ins[h].wait()

        def two(i, _, h=h):
            f2[pl.ds(512 * h + 64 * i, 64), :] = b2[2 * h + i // 4, strip(i % 4, 64), :].astype(F32)
            return 0

        lax.fori_loop(0, 8, two, 0)
        store(f2.at[pl.ds(512 * h, 512)], dw2.at[pl.ds(512 * h, 512)])
    for h in range(2):
        ins[2 + h].wait()

        def one(i, _, h=h):
            at = pl.ds(pl.multiple_of(128 * h + 16 * i, 16), 16)
            for k in range(RANKS):
                for zz in range(RANKS):
                    f1[at, zz * 1024 + k * 256 : zz * 1024 + k * 256 + 256] = b1[k, at, zz * 256 : zz * 256 + 256].astype(F32)
            return 0

        lax.fori_loop(0, 8, one, 0)
        store(f1.at[pl.ds(128 * h, 128)], dw1.at[pl.ds(128 * h, 128)])
    lane = lax.broadcasted_iota(jnp.int32, (16, 128), 1)
    for h in range(2):
        ins[4 + h].wait()

        def attn(i, _, h=h):
            at = pl.ds(pl.multiple_of(128 * h + 16 * i, 16), 16)
            for t in range(3):
                for m in range(2):
                    part = [bq[t, k, at, m * 128 : m * 128 + 128].astype(F32) for k in range(RANKS)]
                    turn = [pltpu.roll(p, HEAD, 1) for p in part]
                    col = t * 1024 + m * 512
                    for g in range(2):
                        a, b = 2 * g, 2 * g + 1
                        fq[at, col + g * 128 : col + g * 128 + 128] = jnp.where(lane < HEAD, part[a], turn[b])
                        fq[at, col + 256 + g * 128 : col + 384 + g * 128] = jnp.where(lane < HEAD, turn[a], part[b])
            return 0

        lax.fori_loop(0, 8, attn, 0)
        store(fq.at[pl.ds(128 * h, 128)], dwq.at[pl.ds(128 * h, 128)])
    ins[6].wait()
    fo[...] = bo[...].astype(F32).reshape(256, 1024)
    store(fo, dwo)
    ins[7].wait()
    f_cg[...] = b_cg[...].astype(F32)
    store(f_cg, cg)
    ins[8].wait()
    for s in range(SLOTS):
        alive = jnp.where(live[0] > s, 1.0, 0.0).astype(F32)
        f_out[s * 64 : s * 64 + 64] = (b_out[s * 64 : s * 64 + 64].astype(F32) * alive).astype(BF16)
    store(f_out, out)
    for cp in outs:
        cp.wait()


def local(
    n_replica,
    clips, cotangent, live_count, w_qkv, w_out, w_fc1, w_fc2, norm_gain, norm_bias, proj_bias, fc1_bias,
):
    vm = pl.BlockSpec(memory_space=pltpu.VMEM)
    smem = pl.BlockSpec(memory_space=pltpu.SMEM)
    anyspace = pl.BlockSpec(memory_space=pl.ANY)
    shape = jax.ShapeDtypeStruct
    tile = (SLOTS, 64, 1024)
    group = (SLOTS, RANKS, 64, 1024)
    V = pltpu.VMEM
    scratch = [
        V(tile, BF16), V(tile, BF16), V(tile, BF16), V((16, 256), F32), V((4, 16, 256), F32), V((12, 256, 128), BF16),
        V((4, 256, 768), BF16), V((4, 64, 1024), BF16), V((4, 256, 1024), BF16), V((4, 256, 1024), BF16),
        V(group, BF16), V(group, BF16), V(group, BF16), V(group, BF16),
        V((3, SLOTS, 256, 256), BF16), V((4, 2, 256, 256), F32), V((SLOTS, 256, 256), BF16),
        V(group, BF16), V(group, BF16), V(group, BF16), V(group, BF16),
        V((8, 64, 1024), BF16), V((8, 64, 1024), BF16), V((8, 64, 1024), BF16), V((8, 64, 1024), BF16),
        V((128, 1024), F32), V((128, 1024), F32), V((SLOTS, 256, 1024), F32), V((SLOTS, 256, 1024), BF16),
        V((SLOTS, 256, 1024), BF16), V((SLOTS, 256, 256), BF16), V((3, SLOTS, 256, 256), BF16),
        V((3, 4, 256, 256), BF16), V((4, 64, 1024), BF16), V((4, 256, 1024), BF16), V((4, 256, 1024), BF16),
        V((3, 4, 128, 256), BF16), V((4, 32, 1024), BF16), V((4, 128, 1024), BF16), V((4, 128, 1024), BF16),
        V((3, 4, 128, 256), BF16), V((4, 32, 1024), BF16), V((4, 128, 1024), BF16), V((4, 128, 1024), BF16),
        V((3, 128, 256), BF16), V((32, 1024), BF16), V((128, 1024), BF16), V((128, 1024), BF16),
        V(tile, BF16), V(tile, BF16), V((16, 1024), F32), V((16, 1024), F32), V((3, 16, 256), F32), V((2, 4, 16, 256), F32),
        V(tile, BF16), V(tile, BF16),
        pltpu.SemaphoreType.DMA((SEMS,)), pltpu.SemaphoreType.DMA((SEMS,)), pltpu.SemaphoreType.DMA((LOADS + 6,)),
    ]
    parts = pl.pallas_call(
        kernel,
        out_shape=(
            shape((128, 1024), BF16), shape((128, 1024), BF16), shape((3, 4, 256, 256), BF16), shape((4, 64, 1024), BF16),
            shape((4, 256, 1024), BF16), shape((4, 256, 1024), BF16), shape((16, 256), F32),
        ),
        in_specs=[vm, vm, smem, vm, vm, vm, vm, anyspace, anyspace, anyspace, anyspace],
        out_specs=(vm, vm, anyspace, anyspace, anyspace, anyspace, vm),
        scratch_shapes=scratch,
        compiler_params=pltpu.CompilerParams(
            collective_id=0, has_side_effects=True, vmem_limit_bytes=60 * 2**20
        ),
        cost_estimate=pl.CostEstimate(flops=10**10, bytes_accessed=2**25, transcendentals=2**21),
    )(clips, cotangent, live_count, norm_gain, norm_bias, proj_bias, fc1_bias, w_qkv, w_out, w_fc1, w_fc2)

    out, clips_grad, *summed = pl.pallas_call(
        finish_kernel,
        out_shape=(
            shape((128, 1024), BF16), shape((128, 1024), F32), shape((256, 3072), F32), shape((256, 1024), F32),
            shape((256, 4096), F32), shape((1024, 1024), F32), shape((2, 256), F32), shape((2, 256), F32),
            shape((4, 256), F32), shape((1024,), F32),
        ),
        in_specs=[smem] + [anyspace] * 6 + [vm],
        out_specs=[anyspace] * 6 + [vm] * 4,
        scratch_shapes=[
            V((128, 1024), BF16), V((128, 1024), BF16), V((3, 4, 256, 256), BF16), V((4, 64, 1024), BF16),
            V((4, 256, 1024), BF16), V((4, 256, 1024), BF16), V((128, 1024), BF16), V((128, 1024), F32),
            V((256, 3072), F32), V((256, 1024), F32), V((256, 4096), F32), V((1024, 1024), F32),
            pltpu.SemaphoreType.DMA((9,)), pltpu.SemaphoreType.DMA((9,)),
        ],
        compiler_params=pltpu.CompilerParams(vmem_limit_bytes=60 * 2**20),
        cost_estimate=pl.CostEstimate(flops=2**22, bytes_accessed=20 * 2**20, transcendentals=0),
    )(live_count, *parts)
    if n_replica > PLANE:
        groups = [list(range(i, n_replica, PLANE)) for i in range(PLANE)]
        summed = lax.psum(tuple(summed), "replica", axis_index_groups=groups)
    return (out.reshape(tile), clips_grad.reshape(tile)) + tuple(summed)


def solution(mesh):
    in_specs = (
        P("replica", "shard", None),
        P("replica", "shard", None),
        P("replica"),
        P("shard", None),
        P("shard", None),
        P("shard", None),
        P("shard", None),
        P(None, "shard"),
        P(None, "shard"),
        P(None, "shard"),
        P("shard"),
    )
    out_specs = (
        P("replica", "shard", None),
        P("replica", "shard", None),
        P("shard", None),
        P("shard", None),
        P("shard", None),
        P("shard", None),
        P(None, "shard"),
        P(None, "shard"),
        P(None, "shard"),
        P("shard"),
    )
    body = functools.partial(local, mesh.shape["replica"])
    return jax.shard_map(body, mesh=mesh, in_specs=in_specs, out_specs=out_specs, check_vma=False)
```

time: 226 us -> 174 us (0.77)
  the two profiles are of different devices: /device:TPU:11 before, /device:TPU:25 now
where the time goes in v2:
time: 174 us; the launch traced here: 173 us
  Pallas kernels  172 us (99%)
    pallas_call x1, Pallas kernels, local(): pl.pallas_call(kernel, out_shape=(shape((128, 1024), BF16), shape((128, 1...  164 us
    pallas_call x1, Pallas kernels, local(): pl.pallas_call(finish_kernel, out_shape=(shape((128, 1024), BF16), shape(...  7.79 us

profile of v2, /device:TPU:25, one launch (start us, length us, event | category | flops | bytes accessed | tf_op | source)
XLA Modules:
  0.0 173.3 jit_solution(12762381804998039874)
XLA Ops:
  1.3 164.2 %shard_map.186 = (bf16[128,1024]{1,0:T(8,128)(2,1)}, bf16[128,1024]{1,0:T(8,128)(2,1)}, bf16[3,4,256,256]{3,2,1,0:T(8,128)(2,1)}, bf16[4,64,1024]{2,1,0:T(8,128)...) custom-call(bf16[2,64,1024]{2,1,0:T(8,128)(2,1)} %clips.1, ...), custom_call_target="tpu_custom_call" | custom-call | flops 10000000000 | bytes 33554432 | tf_op jit(solution)/shard_map/pallas_call | solution.py:787
  165.5 7.8 %shard_map.187 = (bf16[128,1024]{1,0:T(8,128)(2,1)}, f32[128,1024]{1,0:T(8,128)}, f32[256,3072]{1,0:T(8,128)}, f32[256,1024]{1,0:T(8,128)}, f32[256,4096]{1,0:T(...) custom-call(s32[1]{0:T(128)S(6)} %copy.21.live, ...), custom_call_target="tpu_custom_call" | custom-call | flops 4194304 | bytes 20971520 | tf_op jit(solution)/shard_map/pallas_call | solution.py:802

commit v3 on v2

--- a/solution.py
+++ b/solution.py
@@ -15,7 +15,8 @@
 PLANE = 8
 RANKS = 4
 SLOTS = 2
-SEMS = 198
+ARRIVALS = 116
+SENDS = 56
 LOADS = 18
 SCALE = 1.0 / math.sqrt(HEAD)
 
@@ -56,7 +57,7 @@
     n1, n2, dmb, dab, qkv, probs, ob, ab, mb, d2b, d1b, ra, rm, rd2, rd1,
     h1, dh1, slope, gb, dub, dob, dqkv, gq, go, g1, g2,
     cq, co, c1, c2, zq, zo, z1, z2, fq, fo, f1, f2,
-    outb, cgb, sms, smc, smz, smx, outr, cgr,
+    outb, cgb, sms, smc, smz, smx, outr, cgr, total2,
     ssem, rsem, lsem,
 ):
     Z = 4
@@ -81,7 +82,7 @@
 
     px, py, partner = dev(qx, c, z), dev(qy, c, z), dev(q, 1 - c, z)
 
-    counter = [0]
+    counter = [0, 0]
 
     def take(n):
         counter[0] += n
@@ -89,32 +90,44 @@
 
     pending = []
 
-    def send(src, dst, sem, device, when=None, out=None, got=None):
-        done = sem if out is None else out
-
-        def copy():
-            return pltpu.make_async_remote_copy(
-                src, dst, ssem.at[done], rsem.at[sem], device_id=device, device_id_type=MESH
-            )
+    def track(ref, when=None):
+        counter[1] += 1
+        sem = counter[1] - 1
+
+        def finish():
+            pltpu.make_async_remote_copy(
+                ref, ref, ssem.at[sem], rsem.at[0], device_id=partner, device_id_type=MESH
+            ).wait_send()
+
+        pending.append(finish if when is None else lambda: pl.when(when)(finish))
+        return sem
+
+    def send(src, dst, sem, device, out, when=None, got=None):
+        def start():
+            pltpu.make_async_remote_copy(
+                src, dst, ssem.at[out], rsem.at[sem], device_id=device, device_id_type=MESH
+            ).start()
 
         if when is None:
-            copy().start()
-            pending.append(lambda: copy().wait_send())
+            start()
         else:
-            pl.when(when)(lambda: copy().start())
-            pending.append(lambda: pl.when(when)(lambda: copy().wait_send()))
+            pl.when(when)(start)
 
     def arrive(dst, sem):
         pltpu.make_async_remote_copy(
             dst, dst, ssem.at[sem], rsem.at[sem], device_id=partner, device_id_type=MESH
         ).wait_recv()
 
+    def flip(a, b):
+        return (a // 2 + b // 2) % 2 * 2 + (a + b) % 2
+
     def target(s):
-        return (q + z) % RANKS, (q + 2 * s + c) % RANKS
+        plane = (q + 2 * s + c) % RANKS
+        return flip(q, (z + plane) % RANKS), plane
 
     def origin(s):
         a = (z - 2 * s - c + 2 * RANKS) % RANKS
-        return a, (q - a + RANKS) % RANKS
+        return a, (flip(q, a) - z + RANKS) % RANKS
 
     moves = [target(s) for s in range(SLOTS)]
     backs = [origin(s) for s in range(SLOTS)]
@@ -165,7 +178,8 @@
     def exchange(src, dst, sem, places):
         for s in range(SLOTS):
             to = dev(places[s][0], c, places[s][1])
-            send(src.at[s], dst.at[s], sem + s, to, when=jnp.logical_not(stays(places[s])))
+            leaves = jnp.logical_not(stays(places[s]))
+            send(src.at[s], dst.at[s], sem + s, to, track(src.at[s], leaves), when=leaves)
 
             @pl.when(stays(places[s]))
             def _(s=s):
@@ -177,10 +191,10 @@
 
     e_clips, e_cot, e_out, e_cg = take(2), take(2), take(2), take(2)
     exchange(clips, rc, e_clips, moves)
-    s_small = take(3)
+    s_small, o_small = take(1), track(smg.at[pl.ds(0, 3)])
     smg[z] = sml[...]
     for d in range(1, Z):
-        send(sml, smg.at[z], s_small + d - 1, (replica, (z + d) % Z))
+        send(sml, smg.at[z], s_small, (replica, (z + d) % Z), o_small)
     n_first = len(loads)
     for zz in range(RANKS):
         load(w_fc1.at[:, pl.ds(pl.multiple_of(zz * 1024 + q * 256, 256), 256)], w1.at[z, :, pl.ds(zz * 256, 256)])
@@ -192,16 +206,23 @@
     def theirs(half):
         return pl.ds(pl.multiple_of((1 - c) * half, half), half)
 
-    def line_a(w, half, sem):
+    def line(w, half):
+        rows = pl.ds(0, half)
+        return w, half, take(6), (track(w.at[pl.ds(0, 2), rows]), track(w.at[pl.ds(0, 2), rows], middle), track(w.at[pl.ds(0, 3), rows]))
+
+    def line_a(way):
+        w, half, sem, outs = way
         own_part = w.at[z, mine(half)]
-        send(own_part, own_part, sem, (replica, mate))
-        send(own_part, own_part, sem + 1 + z % 2, (replica, far_middle), got=middle)
-
-    def share(w, half, sem, zz, when=None):
+        send(own_part, own_part, sem, (replica, mate), outs[0])
+        send(own_part, own_part, sem + 1 + z % 2, (replica, far_middle), outs[0])
+
+    def share(way, zz, when=None):
+        w, half, sem, outs = way
         part = w.at[zz, mine(half)]
-        send(part, part, sem + 4 + (zz - z + Z) % Z, partner, when=when)
-
-    def line_b(w, half, sem):
+        send(part, part, sem + 2 + (zz - z + Z) % Z, partner, outs[2], when=when)
+
+    def line_b(way):
+        w, half, sem, outs = way
         for f in (lower, 1 - lower):
 
             @pl.when(middle)
@@ -209,92 +230,107 @@
                 arrive(w.at[far + f, mine(half)], sem + 1 + f)
 
             part = w.at[far + f, mine(half)]
-            send(part, part, sem + 1 + f, (replica, mate), when=middle, out=sem + 3 + f, got=end)
-            share(w, half, sem, far + f, when=middle)
-
-    def line_c(w, half, sem):
+            send(part, part, sem + 1 + f, (replica, mate), outs[1], when=middle)
+            share(way, far + f, when=middle)
+
+    def line_c(way):
+        w, half, sem, outs = way
         arrive(w.at[mate, mine(half)], sem)
-        share(w, half, sem, mate)
+        share(way, mate)
         for f in (lower, 1 - lower):
 
             @pl.when(end)
             def _(f=f):
                 arrive(w.at[far + f, mine(half)], sem + 1 + f)
 
-            share(w, half, sem, far + f, when=end)
-
-    def line_d(w, half, sem):
-        for zz in (mate, far + lower, far + 1 - lower):
-            arrive(w.at[zz, theirs(half)], sem + 4 + (zz - z + Z) % Z)
-
-    a_q, a_o, a_1, a_2 = (take(8) for _ in range(4))
+            share(way, far + f, when=end)
+
+    order = (z, mate, far + lower, far + 1 - lower)
+
+    def line_d(way, k):
+        w, half, sem, outs = way
+        arrive(w.at[order[k], theirs(half)], sem + 2 + (order[k] - z + Z) % Z)
+
+    way_q, way_o, way_1, way_2 = line(wq, 128), line(wo, 32), line(w1, 128), line(w2, 128)
 
     CUT = 2
     ROWS = 64 // CUT
 
-    def gather_a(buf, sem):
+    def gather(buf):
+        return buf, take(2 * CUT + 1), track(buf.at[:, pl.ds(0, 3)])
+
+    def gather_a(way):
+        buf, sem, out = way
         for j in range(CUT):
             rows = pl.ds(j * ROWS, ROWS)
-            send(buf.at[0, q, rows], buf.at[0, q, rows], sem + j, px)
-            send(buf.at[1, q, rows], buf.at[1, q, rows], sem + CUT + j, py)
-        send(buf.at[1, q], buf.at[1, q], sem + 2 * CUT, px)
-        send(buf.at[0, q], buf.at[0, q], sem + 2 * CUT + 1, py)
-
-    def gather_b(buf, sem):
+            send(buf.at[0, q, rows], buf.at[0, q, rows], sem + j, px, out)
+            send(buf.at[1, q, rows], buf.at[1, q, rows], sem + CUT + j, py, out)
+        send(buf.at[1, q], buf.at[1, q], sem + 2 * CUT, px, out)
+        send(buf.at[0, q], buf.at[0, q], sem + 2 * CUT, py, out)
+
+    def gather_b(way):
+        buf, sem, out = way
         for j in range(CUT):
             rows = pl.ds(j * ROWS, ROWS)
             arrive(buf.at[0, qx, rows], sem + j)
-            send(buf.at[0, qx, rows], buf.at[0, qx, rows], sem + 2 * CUT + 2 + j, py)
+            send(buf.at[0, qx, rows], buf.at[0, qx, rows], sem + 2 * CUT, py, out)
             arrive(buf.at[1, qy, rows], sem + CUT + j)
-            send(buf.at[1, qy, rows], buf.at[1, qy, rows], sem + 3 * CUT + 2 + j, px)
-
-    def gather_c(buf, sem):
-        arrive(buf.at[1, qx], sem + 2 * CUT)
-        arrive(buf.at[0, qy], sem + 2 * CUT + 1)
-        for j in range(CUT):
-            rows = pl.ds(j * ROWS, ROWS)
-            arrive(buf.at[0, qd, rows], sem + 2 * CUT + 2 + j)
-            arrive(buf.at[1, qd, rows], sem + 3 * CUT + 2 + j)
-
-    def scatter_a(buf, rb, sem):
-        send(buf.at[0, qd], rb.at[0], sem, px)
-        send(buf.at[1, qd], rb.at[1], sem + 1, py)
-        send(buf.at[0, qx], rb.at[2], sem + 2, px)
-        send(buf.at[1, qy], rb.at[3], sem + 3, py)
-
-    def scatter_b(buf, rb, sem):
+            send(buf.at[1, qy, rows], buf.at[1, qy, rows], sem + 2 * CUT, px, out)
+
+    def gather_c(way):
+        buf, sem, out = way
+        arrive(buf.at[0], sem + 2 * CUT)
+
+    def scatter(buf, rb):
+        return buf, rb, take(3), track(rb.at[pl.ds(0, 6)])
+
+    def scatter_a(way):
+        buf, rb, sem, out = way
+        send(buf.at[0, qd], rb.at[0], sem, px, out)
+        send(buf.at[1, qd], rb.at[1], sem + 1, py, out)
+        send(buf.at[0, qx], rb.at[2], sem + 2, px, out)
+        send(buf.at[1, qy], rb.at[3], sem + 2, py, out)
+
+    def scatter_b(way):
+        buf, rb, sem, out = way
         arrive(rb.at[0], sem)
         rb[6] = (buf[0, qy].astype(F32) + rb[0].astype(F32)).astype(BF16)
-        send(rb.at[6], rb.at[4], sem + 4, py)
+        send(rb.at[6], rb.at[4], sem + 2, py, out)
         arrive(rb.at[1], sem + 1)
         rb[7] = (buf[1, qx].astype(F32) + rb[1].astype(F32)).astype(BF16)
-        send(rb.at[7], rb.at[5], sem + 5, px)
-
-    def scatter_c(buf, rb, sem):
-        for k in range(2, 6):
-            arrive(rb.at[k], sem + k)
+        send(rb.at[7], rb.at[5], sem + 2, px, out)
+
+    def scatter_c(way):
+        buf, rb, sem, out = way
+        arrive(rb.at[pl.ds(2, 4)], sem + 2)
         first = buf[0, q].astype(F32) + rb[2].astype(F32) + rb[4].astype(F32)
         second = buf[1, q].astype(F32) + rb[3].astype(F32) + rb[5].astype(F32)
         return jnp.concatenate([first, second], axis=0)
 
-    p_n1, p_n2, p_dm, p_da = (take(4 * CUT + 2) for _ in range(4))
-    p_a, p_m, p_d2, p_d1 = (take(6) for _ in range(4))
+    p_n1, p_n2, p_dm, p_da = (gather(buf) for buf in (n1, n2, dmb, dab))
+    p_a, p_m, p_d2, p_d1 = scatter(ab, ra), scatter(mb, rm), scatter(d2b, rd2), scatter(d1b, rd1)
 
     WAYS = 6
-    t_core = [take(1) for _ in range(WAYS)]
-    t_line = [take(6) for _ in range(WAYS)]
-    t_rank = [take(6) for _ in range(WAYS)]
-    t_pass = [take(1) for _ in range(WAYS)]
-    stored = [None] * WAYS
     halves = (128, 32, 128, 128, 128, 128)
     grads = (gq.at[0], go, g1, g2, gq.at[1], gq.at[2])
     cores = (cq.at[0], co, c1, c2, cq.at[1], cq.at[2])
     lines = (zq.at[0], zo, z1, z2, zq.at[1], zq.at[2])
     finals = (fq.at[0], fo, f1, f2, fq.at[1], fq.at[2])
     results = (oq.at[0], oo, o1, o2, oq.at[1], oq.at[2])
+    t_core = [take(1) for _ in range(WAYS)]
+    t_line = [take(3) for _ in range(WAYS)]
+    t_rank = [take(3) for _ in range(WAYS)]
+    t_pass = [take(1) for _ in range(WAYS)]
+    stored = [None] * WAYS
+    q_core = [track(cores[w]) for w in range(WAYS)]
+    q_line = [track(lines[w].at[pl.ds(0, 3)]) for w in range(WAYS)]
+    q_rank = [track(lines[w].at[pl.ds(0, 3)]) for w in range(WAYS)]
+    q_pass = [track(cores[w]) for w in range(WAYS)]
 
     def reduce_a(w):
-        send(grads[w].at[:, theirs(halves[w])], cores[w], t_core[w], partner)
+        send(grads[w].at[:, theirs(halves[w])], cores[w], t_core[w], partner, q_core[w])
+
+    reach = (1 - lower, lower)
 
     def reduce_b(w):
         rows = mine(halves[w])
@@ -305,20 +341,23 @@
             return 0
 
         lax.fori_loop(0, Z, step, 0)
-        for f in range(2):
-            send(grads[w].at[far + f, rows], lines[w].at[2 + f], t_line[w] + 2 + f, (replica, mate), when=end, got=middle)
-        send(grads[w].at[mate, rows], lines[w].at[0], t_line[w], (replica, mate))
-
-    def reduce_m(w):
+        for f in reach:
+            send(
+                grads[w].at[far + f, rows], lines[w].at[2 + f], t_line[w] + 1 + f, (replica, mate), q_line[w],
+                when=end, got=middle,
+            )
+        send(grads[w].at[mate, rows], lines[w].at[0], t_line[w], (replica, mate), q_line[w])
+
+    def reduce_m(w, k):
         rows = mine(halves[w])
-        for f in range(2):
-
-            @pl.when(middle)
-            def _(f=f):
-                arrive(lines[w].at[2 + f], t_line[w] + 2 + f)
-                grads[w][far + f, rows] = (grads[w][far + f, rows].astype(F32) + lines[w][2 + f].astype(F32)).astype(BF16)
-
-            send(grads[w].at[far + f, rows], lines[w].at[1], t_line[w] + 1, (replica, far + f), when=middle, out=t_line[w] + 4 + f)
+        f = reach[k]
+
+        @pl.when(middle)
+        def _():
+            arrive(lines[w].at[2 + f], t_line[w] + 1 + f)
+            grads[w][far + f, rows] = (grads[w][far + f, rows].astype(F32) + lines[w][2 + f].astype(F32)).astype(BF16)
+
+        send(grads[w].at[far + f, rows], lines[w].at[1], t_line[w], (replica, far + f), q_line[w], when=middle)
 
     def spots(w, rank, core):
         half = halves[w]
@@ -332,37 +371,33 @@
 
     def reduce_c(w):
         half = halves[w]
-        for k in range(2):
-            arrive(lines[w].at[k], t_line[w] + k)
+        arrive(lines[w].at[pl.ds(0, 2)], t_line[w])
         total = grads[w][z, mine(half)].astype(F32)
         for k in range(2):
             total = total + lines[w][k].astype(F32)
         finals[w][...] = total.astype(BF16)
         one, two, both = spots(w, q, c)
         a, b = finals[w].at[pl.ds(0, half // 2)], finals[w].at[pl.ds(half // 2, half // 2)]
-        send(a, one, t_rank[w], px)
-        send(b, two, t_rank[w] + 1, py)
-        send(b, two, t_rank[w] + 2, px)
-        send(a, one, t_rank[w] + 3, py)
+        send(a, one, t_rank[w], px, q_rank[w])
+        send(b, two, t_rank[w] + 1, py, q_rank[w])
+        send(b, two, t_rank[w] + 2, px, q_rank[w])
+        send(a, one, t_rank[w] + 2, py, q_rank[w])
         stored[w] = pltpu.make_async_copy(finals[w], both, lsem.at[LOADS + w])
         stored[w].start()
 
     def reduce_d(w):
         one = spots(w, qx, c)[0]
         arrive(one, t_rank[w])
-        send(one, one, t_rank[w] + 4, py)
+        send(one, one, t_rank[w] + 2, py, q_rank[w])
         two = spots(w, qy, c)[1]
         arrive(two, t_rank[w] + 1)
-        send(two, two, t_rank[w] + 5, px)
+        send(two, two, t_rank[w] + 2, px, q_rank[w])
 
     def reduce_e(w):
-        arrive(spots(w, qx, c)[1], t_rank[w] + 2)
-        arrive(spots(w, qy, c)[0], t_rank[w] + 3)
-        arrive(spots(w, qd, c)[0], t_rank[w] + 4)
-        arrive(spots(w, qd, c)[1], t_rank[w] + 5)
+        arrive(results[w].at[pl.ds(0, 2), mine(halves[w])], t_rank[w] + 2)
         stored[w].wait()
         part = results[w].at[:, mine(halves[w])]
-        send(part, part, t_pass[w], partner)
+        send(part, part, t_pass[w], partner, q_pass[w])
 
     def reduce_f(w):
         arrive(results[w].at[:, theirs(halves[w])], t_pass[w])
@@ -378,14 +413,13 @@
             lo = jnp.where(even, left, pltpu.roll(left, HEAD, 1))
             hi = jnp.where(even, pltpu.roll(right, HEAD, 1), right)
             wq[z, :, t * 256 + m * 128 : t * 256 + m * 128 + 128] = jnp.where(lane < HEAD, lo, hi).astype(BF16)
-    line_a(wq, 128, a_q)
+    line_a(way_q)
 
     for s in range(SLOTS):
         alive = jnp.where(live[0] > s, 1.0, 0.0).astype(F32)
         cm[s] = (cot[s].astype(F32) * alive).astype(BF16)
 
-    for d in range(1, Z):
-        arrive(smg.at[(z - d + Z) % Z], s_small + d - 1)
+    arrive(smg.at[pl.ds(0, 3)], s_small)
 
     def row(i):
         return jnp.concatenate([smg[zz, i : i + 1, :] for zz in range(Z)], axis=1)
@@ -397,18 +431,19 @@
     x = rc[...].astype(F32).reshape(128, 1024)
     xh, _ = normed(x)
     n1[:, q] = (xh * row(0) + row(2)).astype(BF16).reshape(SLOTS, 64, 1024)
-    gather_a(n1, p_n1)
-    gather_b(n1, p_n1)
-    line_b(wq, 128, a_q)
-    line_a(wo, 32, a_o)
+    gather_a(p_n1)
+    gather_b(p_n1)
+    line_b(way_q)
+    line_a(way_o)
     exchange(cm, dmt, e_cot, moves)
-    gather_c(n1, p_n1)
-    line_c(wq, 128, a_q)
-    line_b(wo, 32, a_o)
+    gather_c(p_n1)
+    line_c(way_q)
+    line_b(way_o)
     for cp in loads[n_first:]:
         cp.wait()
-    line_a(w1, 128, a_1)
-    line_d(wq, 128, a_q)
+    line_a(way_1)
+    for k in range(1, Z):
+        line_d(way_q, k)
 
     def qkv_step(t, _):
         bias = jnp.where(t == 0, bias_q, jnp.where(t == 2, bias_v, 0.0))
@@ -417,10 +452,10 @@
         return 0
 
     lax.fori_loop(0, 3, qkv_step, 0)
-    line_c(wo, 32, a_o)
+    line_c(way_o)
     exchange_wait(dmt, e_cot)
     dmb[:, q] = dmt[...]
-    gather_a(dmb, p_dm)
+    gather_a(p_dm)
 
     def attend(i, _):
         s = i // 2
@@ -438,7 +473,8 @@
         return 0
 
     lax.fori_loop(0, 2 * SLOTS, attend, 0)
-    line_d(wo, 32, a_o)
+    for k in range(1, Z):
+        line_d(way_o, k)
 
     def proj_step(s, _):
         val = mm(ob[s], wo[...].reshape(256, 1024))
@@ -446,22 +482,23 @@
         return 0
 
     lax.fori_loop(0, SLOTS, proj_step, 0)
-    scatter_a(ab, ra, p_a)
-    gather_b(dmb, p_dm)
-    scatter_b(ab, ra, p_a)
-    line_b(w1, 128, a_1)
-    line_a(w2, 128, a_2)
-    a = scatter_c(ab, ra, p_a) + row(6)
+    scatter_a(p_a)
+    gather_b(p_dm)
+    scatter_b(p_a)
+    line_b(way_1)
+    line_a(way_2)
+    a = scatter_c(p_a) + row(6)
     hh = x + a
     h1[...] = hh
     xh2, _ = normed(hh)
     n2[:, q] = (xh2 * row(1) + row(3)).astype(BF16).reshape(SLOTS, 64, 1024)
-    gather_a(n2, p_n2)
-    gather_b(n2, p_n2)
-    line_c(w1, 128, a_1)
-    line_b(w2, 128, a_2)
-    line_d(w1, 128, a_1)
-    gather_c(n2, p_n2)
+    gather_a(p_n2)
+    gather_b(p_n2)
+    line_c(way_1)
+    line_b(way_2)
+    for k in range(1, Z):
+        line_d(way_1, k)
+    gather_c(p_n2)
 
     def fc1_step(i, _):
         s = i // RANKS
@@ -474,7 +511,7 @@
         return 0
 
     lax.fori_loop(0, SLOTS * RANKS, fc1_step, 0)
-    gather_c(dmb, p_dm)
+    gather_c(p_dm)
 
     def dw2_step(zz, _):
         g2[zz] = mm_tn(gb[:, :, strip(zz)].reshape(512, 256), dmb[...].reshape(512, 1024)).astype(BF16)
@@ -482,25 +519,30 @@
 
     lax.fori_loop(0, RANKS, dw2_step, 0)
     reduce_a(3)
-    line_c(w2, 128, a_2)
+    line_c(way_2)
     reduce_b(3)
-    line_d(w2, 128, a_2)
-
-    def du_step(zz, _):
+
+    for k in range(RANKS):
+        zz = order[k]
+        if k > 0:
+            line_d(way_2, k)
         cols = strip(zz)
         dg = mm_nt(dmb[...].reshape(512, 1024), w2[zz]).reshape(SLOTS, 256, 256)
-        dub[:, :, cols] = (dg * slope[:, :, cols]).astype(BF16)
-        return 0
-
-    lax.fori_loop(0, RANKS, du_step, 0)
-
-    def dn2_step(zz, _):
-        val = mm_nt(dub[...].reshape(512, 1024), w1[zz])
-        d2b[:, :, :, strip(zz)] = val.astype(BF16).reshape(SLOTS, RANKS, 64, 256)
-        return 0
-
-    lax.fori_loop(0, RANKS, dn2_step, 0)
-    scatter_a(d2b, rd2, p_d2)
+        du = (dg * slope[:, :, cols]).astype(BF16)
+        dub[:, :, cols] = du
+
+        def dn2_step(i, _, k=k, cols=cols):
+            part = mm_nt(dub[:, :, cols].reshape(512, 256), w1[i, :, cols])
+            if k > 0:
+                part = part + total2[i]
+            if k < RANKS - 1:
+                total2[i] = part
+            else:
+                d2b[:, :, :, strip(i)] = part.astype(BF16).reshape(SLOTS, RANKS, 64, 256)
+            return 0
+
+        lax.fori_loop(0, RANKS, dn2_step, 0)
+    scatter_a(p_d2)
 
     def dw1_step(zz, _):
         g1[zz] = mm_tn(n2[:, :, :, strip(zz)].reshape(512, 256), dub[...].reshape(512, 1024)).astype(BF16)
@@ -508,7 +550,7 @@
 
     lax.fori_loop(0, RANKS, dw1_step, 0)
     reduce_a(2)
-    scatter_b(d2b, rd2, p_d2)
+    scatter_b(p_d2)
     reduce_b(2)
 
     sms[...] = jnp.zeros((16, 1024), F32)
@@ -519,12 +561,13 @@
     dy = dmt[...].astype(F32).reshape(128, 1024)
     own(7, dy)
     xh2, inv2 = normed(h1[...])
-    dn2 = scatter_c(d2b, rd2, p_d2)
+    dn2 = scatter_c(p_d2)
     res = dy + norm_back(dn2 * row(1), xh2, inv2)
     da = res.astype(BF16)
     dab[:, q] = da.reshape(SLOTS, 64, 1024)
-    gather_a(dab, p_da)
-    reduce_m(3)
+    gather_a(p_da)
+    for k in range(2):
+        reduce_m(3, k)
     dh1[...] = res
     own(1, dn2 * xh2)
     own(3, dn2)
@@ -537,9 +580,9 @@
         return 0
 
     lax.fori_loop(0, SLOTS, m_step, 0)
-    gather_b(dab, p_da)
-    scatter_a(mb, rm, p_m)
-    gather_c(dab, p_da)
+    gather_b(p_da)
+    scatter_a(p_m)
+    gather_c(p_da)
     go[...] = mm_tn(ob[...].reshape(512, 256), dab[...].reshape(512, 1024)).astype(BF16).reshape(Z, HEAD, 1024)
     reduce_a(1)
 
@@ -568,11 +611,12 @@
         dqkv[2, s, :, cols] = jnp.concatenate(dvs, axis=1).astype(BF16)
         return 0
 
+    reduce_m(2, 0)
     lax.fori_loop(0, SLOTS, attend_back, 0)
-    scatter_b(mb, rm, p_m)
+    scatter_b(p_m)
     reduce_c(3)
+    reduce_m(2, 1)
     lax.fori_loop(SLOTS, 2 * SLOTS, attend_back, 0)
-    reduce_m(2)
 
     def dwq_step(zz, _):
         left = n1[:, :, :, strip(zz)].reshape(512, 256)
@@ -592,14 +636,18 @@
         return 0
 
     lax.fori_loop(0, RANKS, dn1_step, 0)
-    scatter_a(d1b, rd1, p_d1)
+    scatter_a(p_d1)
     for w in (0, 4, 5):
         reduce_b(w)
-    reduce_d(3)
-    m = scatter_c(mb, rm, p_m) + row(7)
+    m = scatter_c(p_m) + row(7)
     outb[...] = (h1[...] + m).astype(BF16).reshape(SLOTS, 64, 1024)
     exchange(outb, outr, e_out, backs)
-    scatter_b(d1b, rd1, p_d1)
+    for k in range(2):
+        reduce_m(1, k)
+    scatter_b(p_d1)
+    reduce_d(3)
+    reduce_m(0, 0)
+    reduce_c(2)
 
     dq_sum = jnp.sum(dqkv[0].astype(F32).reshape(512, 256), axis=0, keepdims=True)
     dv_sum = jnp.sum(dqkv[2].astype(F32).reshape(512, 256), axis=0, keepdims=True)
@@ -610,44 +658,45 @@
         pieces += [dq_sum[:, h], dv_sum[:, h], gap]
     sms[pl.ds(8 + 2 * q, 1), :] = jnp.concatenate(pieces, axis=1)
     xh, inv = normed(rc[...].astype(F32).reshape(128, 1024))
-    reduce_m(1)
-    reduce_m(0)
-    reduce_m(4)
-    reduce_c(2)
-
-    dn1 = scatter_c(d1b, rd1, p_d1)
+    reduce_m(0, 1)
+    reduce_m(4, 0)
+    reduce_c(1)
+
+    dn1 = scatter_c(p_d1)
     own(0, dn1 * xh)
     own(2, dn1)
-    u_core, u_line, u_rank = take(1), take(3), take(3)
-    send(sms, smc, u_core, partner)
+    u_core, u_line, u_rank = take(1), take(1), take(1)
+    send(sms, smc, u_core, partner, track(sms))
     cgb[...] = (dh1[...] + norm_back(dn1 * row(0), xh, inv)).astype(BF16).reshape(SLOTS, 64, 1024)
     exchange(cgb, cgr, e_cg, backs)
+    reduce_m(4, 1)
+    reduce_c(0)
+    reduce_m(5, 0)
+    reduce_m(5, 1)
 
     arrive(smc, u_core)
     both = sms[...] + smc[...]
     for zz in range(Z):
         smx[0, zz] = both[:, zz * 256 : zz * 256 + 256]
+    o_line, o_rank = track(smz), track(smz)
     for d in range(1, Z):
-        send(smx.at[0, (z + d) % Z], smz.at[d - 1], u_line + d - 1, (replica, (z + d) % Z))
-    reduce_m(5)
-    reduce_c(1)
-    reduce_c(0)
+        send(smx.at[0, (z + d) % Z], smz.at[d - 1], u_line, (replica, (z + d) % Z), o_line)
     reduce_d(2)
+    reduce_c(4)
     reduce_e(3)
-    reduce_c(4)
+    reduce_d(1)
     reduce_c(5)
+    reduce_d(0)
+    reduce_d(4)
     reduce_e(2)
-    for d in range(Z - 1):
-        arrive(smz.at[d], u_line + d)
+    arrive(smz, u_line)
     smx[1, 0] = smx[0, z] + smz[0] + smz[1] + smz[2]
     for k, rank in enumerate((qx, qy, qd)):
-        send(smx.at[1, 0], smx.at[1, 1 + k], u_rank + k, dev(rank, c, z))
-    for w in (1, 0, 4, 5):
-        reduce_d(w)
+        send(smx.at[1, 0], smx.at[1, 1 + k], u_rank, dev(rank, c, z), o_rank)
+    reduce_d(5)
     for w in (1, 0, 4, 5):
         reduce_e(w)
-    for k in range(RANKS - 1):
-        arrive(smx.at[1, 1 + k], u_rank + k)
+    arrive(smx.at[1, pl.ds(1, 3)], u_rank)
     sm_out[...] = smx[1, 0] + smx[1, 1] + smx[1, 2] + smx[1, 3]
 
     exchange_wait(outr, e_out)
@@ -656,7 +705,7 @@
     cg_k[...] = cgr[...].reshape(128, 1024)
     for w in (3, 2, 1, 0, 4, 5):
         reduce_f(w)
-    assert counter[0] <= SEMS, counter[0]
+    assert counter == [ARRIVALS, SENDS], counter
     for finish in pending:
         finish()
 
@@ -781,8 +830,8 @@
         V((3, 4, 128, 256), BF16), V((4, 32, 1024), BF16), V((4, 128, 1024), BF16), V((4, 128, 1024), BF16),
         V((3, 128, 256), BF16), V((32, 1024), BF16), V((128, 1024), BF16), V((128, 1024), BF16),
         V(tile, BF16), V(tile, BF16), V((16, 1024), F32), V((16, 1024), F32), V((3, 16, 256), F32), V((2, 4, 16, 256), F32),
-        V(tile, BF16), V(tile, BF16),
-        pltpu.SemaphoreType.DMA((SEMS,)), pltpu.SemaphoreType.DMA((SEMS,)), pltpu.SemaphoreType.DMA((LOADS + 6,)),
+        V(tile, BF16), V(tile, BF16), V((4, 512, 256), F32),
+        pltpu.SemaphoreType.DMA((SENDS,)), pltpu.SemaphoreType.DMA((ARRIVALS,)), pltpu.SemaphoreType.DMA((LOADS + 6,)),
     ]
     parts = pl.pallas_call(
         kernel,

time: 174 us -> 168 us (0.966)
  the two profiles are of different devices: /device:TPU:25 before, /device:TPU:0 now
where the time goes in v3:
time: 168 us
  Pallas kernels  166 us (99%)
    pallas_call x1, Pallas kernels, local(): pl.pallas_call(kernel, out_shape=(shape((128, 1024), BF16), shape((128, 1...  159 us
    pallas_call x1, Pallas kernels, local(): pl.pallas_call(finish_kernel, out_shape=(shape((128, 1024), BF16), shape(...  7.79 us

profile of v3, /device:TPU:0, one launch (start us, length us, event | category | flops | bytes accessed | tf_op | source)
XLA Modules:
  0.0 167.7 jit_solution(2458406191453360836)
XLA Ops:
  1.3 158.6 %shard_map.186 = (bf16[128,1024]{1,0:T(8,128)(2,1)}, bf16[128,1024]{1,0:T(8,128)(2,1)}, bf16[3,4,256,256]{3,2,1,0:T(8,128)(2,1)}, bf16[4,64,1024]{2,1,0:T(8,128)...) custom-call(bf16[2,64,1024]{2,1,0:T(8,128)(2,1)} %clips.1, ...), custom_call_target="tpu_custom_call" | custom-call | flops 10000000000 | bytes 33554432 | tf_op jit(solution)/shard_map/pallas_call | solution.py:836
  159.9 7.8 %shard_map.187 = (bf16[128,1024]{1,0:T(8,128)(2,1)}, f32[128,1024]{1,0:T(8,128)}, f32[256,3072]{1,0:T(8,128)}, f32[256,1024]{1,0:T(8,128)}, f32[256,4096]{1,0:T(...) custom-call(s32[1]{0:T(128)S(6)} %copy.21.live, ...), custom_call_target="tpu_custom_call" | custom-call | flops 4194304 | bytes 20971520 | tf_op jit(solution)/shard_map/pallas_call | solution.py:851

commit v4 on v3

--- a/solution.py
+++ b/solution.py
@@ -15,9 +15,9 @@
 PLANE = 8
 RANKS = 4
 SLOTS = 2
-ARRIVALS = 116
-SENDS = 56
-LOADS = 18
+ARRIVALS = 128
+SENDS = 62
+LOADS = 19
 SCALE = 1.0 / math.sqrt(HEAD)
 
 
@@ -51,13 +51,13 @@
 
 
 def kernel(
-    clips, cot, live, gains, nbias, pbias, fbias, w_qkv, w_out, w_fc1, w_fc2,
+    clips, cotangent, live, gains, nbias, pbias, fbias, w_qkv, w_out, w_fc1, w_fc2,
     out_k, cg_k, oq, oo, o1, o2, sm_out,
-    rc, cm, dmt, sml, smg, tmp, wq, wo, w1, w2,
+    cot, rc, cm, dmt, sml, smg, tmp, wq, wo, w1, w2,
     n1, n2, dmb, dab, qkv, probs, ob, ab, mb, d2b, d1b, ra, rm, rd2, rd1,
     h1, dh1, slope, gb, dub, dob, dqkv, gq, go, g1, g2,
     cq, co, c1, c2, zq, zo, z1, z2, fq, fo, f1, f2,
-    outb, cgb, sms, smc, smz, smx, outr, cgr, total2,
+    outb, cgb, sms, smc, smz, smx, total2,
     ssem, rsem, lsem,
 ):
     Z = 4
@@ -147,6 +147,7 @@
         for zz in range(RANKS):
             load(w_qkv.at[:, pl.ds(pl.multiple_of(t * 1024 + zz * 256 + pair, 128), 128)], tmp.at[t * RANKS + zz])
     load(w_out.at[strip(q, HEAD), :], wo.at[z])
+    load(cotangent, cot)
 
     barrier = pltpu.get_barrier_semaphore()
     for device in (px, py, dev(qd, c, z), partner):
@@ -251,7 +252,10 @@
         w, half, sem, outs = way
         arrive(w.at[order[k], theirs(half)], sem + 2 + (order[k] - z + Z) % Z)
 
-    way_q, way_o, way_1, way_2 = line(wq, 128), line(wo, 32), line(w1, 128), line(w2, 128)
+    ways_q = [line(wq.at[:, :, pl.ds(t * 256, 256)], 128) for t in range(3)]
+    way_o = line(wo, 32)
+    ways_1 = [line(w1.at[:, :, pl.ds(0, 1024)], 128) for t in range(1)]
+    ways_2 = [line(w2.at[:, :, pl.ds(0, 1024)], 128) for t in range(1)]
 
     CUT = 2
     ROWS = 64 // CUT
@@ -413,7 +417,8 @@
             lo = jnp.where(even, left, pltpu.roll(left, HEAD, 1))
             hi = jnp.where(even, pltpu.roll(right, HEAD, 1), right)
             wq[z, :, t * 256 + m * 128 : t * 256 + m * 128 + 128] = jnp.where(lane < HEAD, lo, hi).astype(BF16)
-    line_a(way_q)
+    for way in ways_q:
+        line_a(way)
 
     for s in range(SLOTS):
         alive = jnp.where(live[0] > s, 1.0, 0.0).astype(F32)
@@ -432,18 +437,23 @@
     xh, _ = normed(x)
     n1[:, q] = (xh * row(0) + row(2)).astype(BF16).reshape(SLOTS, 64, 1024)
     gather_a(p_n1)
+    line_b(ways_q[0])
     gather_b(p_n1)
-    line_b(way_q)
+    line_b(ways_q[1])
+    line_b(ways_q[2])
     line_a(way_o)
     exchange(cm, dmt, e_cot, moves)
     gather_c(p_n1)
-    line_c(way_q)
+    for way in ways_q:
+        line_c(way)
     line_b(way_o)
     for cp in loads[n_first:]:
         cp.wait()
-    line_a(way_1)
-    for k in range(1, Z):
-        line_d(way_q, k)
+    for way in ways_1:
+        line_a(way)
+    for way in ways_q:
+        for k in range(1, Z):
+            line_d(way, k)
 
     def qkv_step(t, _):
         bias = jnp.where(t == 0, bias_q, jnp.where(t == 2, bias_v, 0.0))
@@ -485,8 +495,10 @@
     scatter_a(p_a)
     gather_b(p_dm)
     scatter_b(p_a)
-    line_b(way_1)
-    line_a(way_2)
+    for way in ways_1:
+        line_b(way)
+    for way in ways_2:
+        line_a(way)
     a = scatter_c(p_a) + row(6)
     hh = x + a
     h1[...] = hh
@@ -494,10 +506,13 @@
     n2[:, q] = (xh2 * row(1) + row(3)).astype(BF16).reshape(SLOTS, 64, 1024)
     gather_a(p_n2)
     gather_b(p_n2)
-    line_c(way_1)
-    line_b(way_2)
-    for k in range(1, Z):
-        line_d(way_1, k)
+    for way in ways_1:
+        line_c(way)
+    for way in ways_2:
+        line_b(way)
+    for way in ways_1:
+        for k in range(1, Z):
+            line_d(way, k)
     gather_c(p_n2)
 
     def fc1_step(i, _):
@@ -519,13 +534,16 @@
 
     lax.fori_loop(0, RANKS, dw2_step, 0)
     reduce_a(3)
-    line_c(way_2)
-    reduce_b(3)
+    for way in ways_2:
+        line_c(way)
 
     for k in range(RANKS):
         zz = order[k]
+        if k == 1:
+            reduce_b(3)
         if k > 0:
-            line_d(way_2, k)
+            for way in ways_2:
+                line_d(way, k)
         cols = strip(zz)
         dg = mm_nt(dmb[...].reshape(512, 1024), w2[zz]).reshape(SLOTS, 256, 256)
         du = (dg * slope[:, :, cols]).astype(BF16)
@@ -618,16 +636,6 @@
     reduce_m(2, 1)
     lax.fori_loop(SLOTS, 2 * SLOTS, attend_back, 0)
 
-    def dwq_step(zz, _):
-        left = n1[:, :, :, strip(zz)].reshape(512, 256)
-        for t in range(3):
-            gq[t, zz] = mm_tn(left, dqkv[t].reshape(512, 256)).astype(BF16)
-        return 0
-
-    lax.fori_loop(0, RANKS, dwq_step, 0)
-    for w in (0, 4, 5):
-        reduce_a(w)
-
     def dn1_step(zz, _):
         val = mm_nt(dqkv[0].reshape(512, 256), wq[zz, :, 0:256])
         val = val + mm_nt(dqkv[1].reshape(512, 256), wq[zz, :, 256:512])
@@ -637,17 +645,33 @@
 
     lax.fori_loop(0, RANKS, dn1_step, 0)
     scatter_a(p_d1)
+    def dwq_step(zz, _):
+        left = n1[:, :, :, strip(zz)].reshape(512, 256)
+        for t in range(3):
+            gq[t, zz] = mm_tn(left, dqkv[t].reshape(512, 256)).astype(BF16)
+        return 0
+
+    lax.fori_loop(0, RANKS, dwq_step, 0)
     for w in (0, 4, 5):
-        reduce_b(w)
-    m = scatter_c(p_m) + row(7)
-    outb[...] = (h1[...] + m).astype(BF16).reshape(SLOTS, 64, 1024)
-    exchange(outb, outr, e_out, backs)
+        reduce_a(w)
+
     for k in range(2):
         reduce_m(1, k)
     scatter_b(p_d1)
+    for w in (0, 4, 5):
+        reduce_b(w)
     reduce_d(3)
-    reduce_m(0, 0)
+    m = scatter_c(p_m) + row(7)
+    outb[...] = (h1[...] + m).astype(BF16).reshape(SLOTS, 64, 1024)
+    xh, inv = normed(rc[...].astype(F32).reshape(128, 1024))
+
+    dn1 = scatter_c(p_d1)
+    cgb[...] = (dh1[...] + norm_back(dn1 * row(0), xh, inv)).astype(BF16).reshape(SLOTS, 64, 1024)
+    exchange(cgb, cg_k, e_cg, backs)
     reduce_c(2)
+    exchange(outb, out_k, e_out, backs)
+    own(0, dn1 * xh)
+    own(2, dn1)
 
     dq_sum = jnp.sum(dqkv[0].astype(F32).reshape(512, 256), axis=0, keepdims=True)
     dv_sum = jnp.sum(dqkv[2].astype(F32).reshape(512, 256), axis=0, keepdims=True)
@@ -657,23 +681,12 @@
         h = slice(zz * HEAD, zz * HEAD + HEAD)
         pieces += [dq_sum[:, h], dv_sum[:, h], gap]
     sms[pl.ds(8 + 2 * q, 1), :] = jnp.concatenate(pieces, axis=1)
-    xh, inv = normed(rc[...].astype(F32).reshape(128, 1024))
-    reduce_m(0, 1)
-    reduce_m(4, 0)
-    reduce_c(1)
-
-    dn1 = scatter_c(p_d1)
-    own(0, dn1 * xh)
-    own(2, dn1)
     u_core, u_line, u_rank = take(1), take(1), take(1)
     send(sms, smc, u_core, partner, track(sms))
-    cgb[...] = (dh1[...] + norm_back(dn1 * row(0), xh, inv)).astype(BF16).reshape(SLOTS, 64, 1024)
-    exchange(cgb, cgr, e_cg, backs)
-    reduce_m(4, 1)
-    reduce_c(0)
-    reduce_m(5, 0)
-    reduce_m(5, 1)
-
+    for k in range(2):
+        reduce_m(0, k)
+    reduce_c(1)
+    reduce_e(3)
     arrive(smc, u_core)
     both = sms[...] + smc[...]
     for zz in range(Z):
@@ -681,14 +694,18 @@
     o_line, o_rank = track(smz), track(smz)
     for d in range(1, Z):
         send(smx.at[0, (z + d) % Z], smz.at[d - 1], u_line, (replica, (z + d) % Z), o_line)
+    for k in range(2):
+        reduce_m(4, k)
+    reduce_c(0)
+    for k in range(2):
+        reduce_m(5, k)
     reduce_d(2)
     reduce_c(4)
-    reduce_e(3)
     reduce_d(1)
     reduce_c(5)
     reduce_d(0)
+    reduce_e(2)
     reduce_d(4)
-    reduce_e(2)
     arrive(smz, u_line)
     smx[1, 0] = smx[0, z] + smz[0] + smz[1] + smz[2]
     for k, rank in enumerate((qx, qy, qd)):
@@ -699,10 +716,8 @@
     arrive(smx.at[1, pl.ds(1, 3)], u_rank)
     sm_out[...] = smx[1, 0] + smx[1, 1] + smx[1, 2] + smx[1, 3]
 
-    exchange_wait(outr, e_out)
-    out_k[...] = outr[...].reshape(128, 1024)
-    exchange_wait(cgr, e_cg)
-    cg_k[...] = cgr[...].reshape(128, 1024)
+    exchange_wait(out_k, e_out)
+    exchange_wait(cg_k, e_cg)
     for w in (3, 2, 1, 0, 4, 5):
         reduce_f(w)
     assert counter == [ARRIVALS, SENDS], counter
@@ -794,12 +809,12 @@
     fo[...] = bo[...].astype(F32).reshape(256, 1024)
     store(fo, dwo)
     ins[7].wait()
-    f_cg[...] = b_cg[...].astype(F32)
+    f_cg[...] = b_cg[...].astype(F32).reshape(128, 1024)
     store(f_cg, cg)
     ins[8].wait()
     for s in range(SLOTS):
         alive = jnp.where(live[0] > s, 1.0, 0.0).astype(F32)
-        f_out[s * 64 : s * 64 + 64] = (b_out[s * 64 : s * 64 + 64].astype(F32) * alive).astype(BF16)
+        f_out[s * 64 : s * 64 + 64] = (b_out[s].astype(F32) * alive).astype(BF16)
     store(f_out, out)
     for cp in outs:
         cp.wait()
@@ -817,7 +832,7 @@
     group = (SLOTS, RANKS, 64, 1024)
     V = pltpu.VMEM
     scratch = [
-        V(tile, BF16), V(tile, BF16), V(tile, BF16), V((16, 256), F32), V((4, 16, 256), F32), V((12, 256, 128), BF16),
+        V(tile, BF16), V(tile, BF16), V(tile, BF16), V(tile, BF16), V((16, 256), F32), V((4, 16, 256), F32), V((12, 256, 128), BF16),
         V((4, 256, 768), BF16), V((4, 64, 1024), BF16), V((4, 256, 1024), BF16), V((4, 256, 1024), BF16),
         V(group, BF16), V(group, BF16), V(group, BF16), V(group, BF16),
         V((3, SLOTS, 256, 256), BF16), V((4, 2, 256, 256), F32), V((SLOTS, 256, 256), BF16),
@@ -830,17 +845,17 @@
         V((3, 4, 128, 256), BF16), V((4, 32, 1024), BF16), V((4, 128, 1024), BF16), V((4, 128, 1024), BF16),
         V((3, 128, 256), BF16), V((32, 1024), BF16), V((128, 1024), BF16), V((128, 1024), BF16),
         V(tile, BF16), V(tile, BF16), V((16, 1024), F32), V((16, 1024), F32), V((3, 16, 256), F32), V((2, 4, 16, 256), F32),
-        V(tile, BF16), V(tile, BF16), V((4, 512, 256), F32),
+        V((4, 512, 256), F32),
         pltpu.SemaphoreType.DMA((SENDS,)), pltpu.SemaphoreType.DMA((ARRIVALS,)), pltpu.SemaphoreType.DMA((LOADS + 6,)),
     ]
     parts = pl.pallas_call(
         kernel,
         out_shape=(
-            shape((128, 1024), BF16), shape((128, 1024), BF16), shape((3, 4, 256, 256), BF16), shape((4, 64, 1024), BF16),
+            shape(tile, BF16), shape(tile, BF16), shape((3, 4, 256, 256), BF16), shape((4, 64, 1024), BF16),
             shape((4, 256, 1024), BF16), shape((4, 256, 1024), BF16), shape((16, 256), F32),
         ),
-        in_specs=[vm, vm, smem, vm, vm, vm, vm, anyspace, anyspace, anyspace, anyspace],
-        out_specs=(vm, vm, anyspace, anyspace, anyspace, anyspace, vm),
+        in_specs=[anyspace, anyspace, smem, vm, vm, vm, vm, anyspace, anyspace, anyspace, anyspace],
+        out_specs=(anyspace, anyspace, anyspace, anyspace, anyspace, anyspace, vm),
         scratch_shapes=scratch,
         compiler_params=pltpu.CompilerParams(
             collective_id=0, has_side_effects=True, vmem_limit_bytes=60 * 2**20
@@ -858,7 +873,7 @@
         in_specs=[smem] + [anyspace] * 6 + [vm],
         out_specs=[anyspace] * 6 + [vm] * 4,
         scratch_shapes=[
-            V((128, 1024), BF16), V((128, 1024), BF16), V((3, 4, 256, 256), BF16), V((4, 64, 1024), BF16),
+            V(tile, BF16), V(tile, BF16), V((3, 4, 256, 256), BF16), V((4, 64, 1024), BF16),
             V((4, 256, 1024), BF16), V((4, 256, 1024), BF16), V((128, 1024), BF16), V((128, 1024), F32),
             V((256, 3072), F32), V((256, 1024), F32), V((256, 4096), F32), V((1024, 1024), F32),
             pltpu.SemaphoreType.DMA((9,)), pltpu.SemaphoreType.DMA((9,)),

time: 168 us -> 165 us (0.982)
  Pallas kernels: 166 us -> 163 us
    pallas_call x1, Pallas kernels: 159 us -> 155 us  [local(): pl.pallas_call(kernel, out_shape=(shape(tile, BF16), shape(tile, BF16), s...]
where the time goes in v4:
time: 165 us
  Pallas kernels  163 us (99%)
    pallas_call x1, Pallas kernels, local(): pl.pallas_call(kernel, out_shape=(shape(tile, BF16), shape(tile, BF16), s...  155 us
    pallas_call x1, Pallas kernels, local(): pl.pallas_call(finish_kernel, out_shape=(shape((128, 1024), BF16), shape(...  7.79 us

profile of v4, /device:TPU:0, one launch (start us, length us, event | category | flops | bytes accessed | tf_op | source)
XLA Modules:
  0.0 164.6 jit_solution(11040729058747946731)
XLA Ops:
  1.3 155.5 %shard_map.186 = (bf16[2,64,1024]{2,1,0:T(8,128)(2,1)}, bf16[2,64,1024]{2,1,0:T(8,128)(2,1)}, bf16[3,4,256,256]{3,2,1,0:T(8,128)(2,1)}, bf16[4,64,1024]{2,1,0:T(...) custom-call(bf16[2,64,1024]{2,1,0:T(8,128)(2,1)} %clips.1, ...), custom_call_target="tpu_custom_call" | custom-call | flops 10000000000 | bytes 33554432 | tf_op jit(solution)/shard_map/pallas_call | solution.py:851
  156.8 7.8 %shard_map.187 = (bf16[128,1024]{1,0:T(8,128)(2,1)}, f32[128,1024]{1,0:T(8,128)}, f32[256,3072]{1,0:T(8,128)}, f32[256,1024]{1,0:T(8,128)}, f32[256,4096]{1,0:T(...) custom-call(s32[1]{0:T(128)S(6)} %copy.21.live, ...), custom_call_target="tpu_custom_call" | custom-call | flops 4194304 | bytes 20971520 | tf_op jit(solution)/shard_map/pallas_call | solution.py:866

commit v5 on v4

--- a/solution.py
+++ b/solution.py
@@ -88,9 +88,9 @@
         counter[0] += n
         return counter[0] - n
 
-    pending = []
-
-    def track(ref, when=None):
+    early, pending = [], []
+
+    def track(ref, when=None, into=pending):
         counter[1] += 1
         sem = counter[1] - 1
 
@@ -99,7 +99,7 @@
                 ref, ref, ssem.at[sem], rsem.at[0], device_id=partner, device_id_type=MESH
             ).wait_send()
 
-        pending.append(finish if when is None else lambda: pl.when(when)(finish))
+        into.append(finish if when is None else lambda: pl.when(when)(finish))
         return sem
 
     def send(src, dst, sem, device, out, when=None, got=None):
@@ -176,11 +176,11 @@
 
     pl.semaphore_wait(barrier, count)
 
-    def exchange(src, dst, sem, places):
+    def exchange(src, dst, sem, places, into=pending):
         for s in range(SLOTS):
             to = dev(places[s][0], c, places[s][1])
             leaves = jnp.logical_not(stays(places[s]))
-            send(src.at[s], dst.at[s], sem + s, to, track(src.at[s], leaves), when=leaves)
+            send(src.at[s], dst.at[s], sem + s, to, track(src.at[s], leaves, into), when=leaves)
 
             @pl.when(stays(places[s]))
             def _(s=s):
@@ -191,8 +191,8 @@
             arrive(dst.at[s], sem + s)
 
     e_clips, e_cot, e_out, e_cg = take(2), take(2), take(2), take(2)
-    exchange(clips, rc, e_clips, moves)
-    s_small, o_small = take(1), track(smg.at[pl.ds(0, 3)])
+    exchange(clips, rc, e_clips, moves, early)
+    s_small, o_small = take(1), track(smg.at[pl.ds(0, 3)], None, early)
     smg[z] = sml[...]
     for d in range(1, Z):
         send(sml, smg.at[z], s_small, (replica, (z + d) % Z), o_small)
@@ -209,7 +209,10 @@
 
     def line(w, half):
         rows = pl.ds(0, half)
-        return w, half, take(6), (track(w.at[pl.ds(0, 2), rows]), track(w.at[pl.ds(0, 2), rows], middle), track(w.at[pl.ds(0, 3), rows]))
+        own_sends = track(w.at[pl.ds(0, 2), rows], None, early)
+        passed_on = track(w.at[pl.ds(0, 2), rows], middle, early)
+        shared = track(w.at[pl.ds(0, 3), rows], None, early)
+        return w, half, take(6), (own_sends, passed_on, shared)
 
     def line_a(way):
         w, half, sem, outs = way
@@ -261,7 +264,7 @@
     ROWS = 64 // CUT
 
     def gather(buf):
-        return buf, take(2 * CUT + 1), track(buf.at[:, pl.ds(0, 3)])
+        return buf, take(2 * CUT + 1), track(buf.at[:, pl.ds(0, 3)], None, early)
 
     def gather_a(way):
         buf, sem, out = way
@@ -286,7 +289,7 @@
         arrive(buf.at[0], sem + 2 * CUT)
 
     def scatter(buf, rb):
-        return buf, rb, take(3), track(rb.at[pl.ds(0, 6)])
+        return buf, rb, take(3), track(rb.at[pl.ds(0, 6)], None, pending if buf is d1b else early)
 
     def scatter_a(way):
         buf, rb, sem, out = way
@@ -442,7 +445,7 @@
     line_b(ways_q[1])
     line_b(ways_q[2])
     line_a(way_o)
-    exchange(cm, dmt, e_cot, moves)
+    exchange(cm, dmt, e_cot, moves, early)
     gather_c(p_n1)
     for way in ways_q:
         line_c(way)
@@ -467,7 +470,7 @@
     dmb[:, q] = dmt[...]
     gather_a(p_dm)
 
-    def attend(i, _):
+    def attend_pair(i):
         s = i // 2
         cols = strip(i % 2, 128)
         qq, kk, vv = qkv[0, s, :, cols], qkv[1, s, :, cols], qkv[2, s, :, cols]
@@ -476,13 +479,17 @@
             h = slice(j * HEAD, j * HEAD + HEAD)
             score = mm_nt(qq[:, h], kk[:, h]) * SCALE
             e = jnp.exp(score - jnp.max(score, axis=-1, keepdims=True))
-            p = e / jnp.sum(e, axis=-1, keepdims=True)
+            p = e * (1.0 / jnp.sum(e, axis=-1, keepdims=True))
             probs[i, j] = p
             outs.append(mm(p.astype(BF16), vv[:, h]))
         ob[s, :, cols] = jnp.concatenate(outs, axis=1).astype(BF16)
-        return 0
-
-    lax.fori_loop(0, 2 * SLOTS, attend, 0)
+
+    def attend(s, _):
+        attend_pair(2 * s)
+        attend_pair(2 * s + 1)
+        return 0
+
+    lax.fori_loop(0, SLOTS, attend, 0)
     for k in range(1, Z):
         line_d(way_o, k)
 
@@ -561,6 +568,13 @@
 
         lax.fori_loop(0, RANKS, dn2_step, 0)
     scatter_a(p_d2)
+    def m_step(s, _):
+        mb[s] = mm(gb[s], w2[...].reshape(1024, 1024)).astype(BF16).reshape(RANKS, 64, 1024)
+        return 0
+
+    lax.fori_loop(0, SLOTS, m_step, 0)
+    scatter_b(p_d2)
+    scatter_a(p_m)
 
     def dw1_step(zz, _):
         g1[zz] = mm_tn(n2[:, :, :, strip(zz)].reshape(512, 256), dub[...].reshape(512, 1024)).astype(BF16)
@@ -568,7 +582,6 @@
 
     lax.fori_loop(0, RANKS, dw1_step, 0)
     reduce_a(2)
-    scatter_b(p_d2)
     reduce_b(2)
 
     sms[...] = jnp.zeros((16, 1024), F32)
@@ -593,13 +606,8 @@
     fc1_sum = jnp.sum(dub[...].astype(F32).reshape(512, 1024), axis=0, keepdims=True)
     sms[pl.ds(9 + 2 * q, 1), :] = fc1_sum
 
-    def m_step(s, _):
-        mb[s] = mm(gb[s], w2[...].reshape(1024, 1024)).astype(BF16).reshape(RANKS, 64, 1024)
-        return 0
-
-    lax.fori_loop(0, SLOTS, m_step, 0)
     gather_b(p_da)
-    scatter_a(p_m)
+    scatter_b(p_m)
     gather_c(p_da)
     go[...] = mm_tn(ob[...].reshape(512, 256), dab[...].reshape(512, 1024)).astype(BF16).reshape(Z, HEAD, 1024)
     reduce_a(1)
@@ -631,7 +639,9 @@
 
     reduce_m(2, 0)
     lax.fori_loop(0, SLOTS, attend_back, 0)
-    scatter_b(p_m)
+    m = scatter_c(p_m) + row(7)
+    outb[...] = (h1[...] + m).astype(BF16).reshape(SLOTS, 64, 1024)
+    exchange(outb, out_k, e_out, backs)
     reduce_c(3)
     reduce_m(2, 1)
     lax.fori_loop(SLOTS, 2 * SLOTS, attend_back, 0)
@@ -657,22 +667,6 @@
 
     for k in range(2):
         reduce_m(1, k)
-    scatter_b(p_d1)
-    for w in (0, 4, 5):
-        reduce_b(w)
-    reduce_d(3)
-    m = scatter_c(p_m) + row(7)
-    outb[...] = (h1[...] + m).astype(BF16).reshape(SLOTS, 64, 1024)
-    xh, inv = normed(rc[...].astype(F32).reshape(128, 1024))
-
-    dn1 = scatter_c(p_d1)
-    cgb[...] = (dh1[...] + norm_back(dn1 * row(0), xh, inv)).astype(BF16).reshape(SLOTS, 64, 1024)
-    exchange(cgb, cg_k, e_cg, backs)
-    reduce_c(2)
-    exchange(outb, out_k, e_out, backs)
-    own(0, dn1 * xh)
-    own(2, dn1)
-
     dq_sum = jnp.sum(dqkv[0].astype(F32).reshape(512, 256), axis=0, keepdims=True)
     dv_sum = jnp.sum(dqkv[2].astype(F32).reshape(512, 256), axis=0, keepdims=True)
     gap = jnp.zeros((1, 128), F32)
@@ -681,11 +675,27 @@
         h = slice(zz * HEAD, zz * HEAD + HEAD)
         pieces += [dq_sum[:, h], dv_sum[:, h], gap]
     sms[pl.ds(8 + 2 * q, 1), :] = jnp.concatenate(pieces, axis=1)
+    scatter_b(p_d1)
+    reduce_c(2)
+    for w in (0, 4, 5):
+        reduce_b(w)
+    reduce_d(3)
+    xh, inv = normed(rc[...].astype(F32).reshape(128, 1024))
+
+    dn1 = scatter_c(p_d1)
+    cgb[...] = (dh1[...] + norm_back(dn1 * row(0), xh, inv)).astype(BF16).reshape(SLOTS, 64, 1024)
+    exchange(cgb, cg_k, e_cg, backs)
+    own(0, dn1 * xh)
+    own(2, dn1)
+
     u_core, u_line, u_rank = take(1), take(1), take(1)
     send(sms, smc, u_core, partner, track(sms))
     for k in range(2):
         reduce_m(0, k)
+    for k in range(2):
+        reduce_m(4, k)
     reduce_c(1)
+    reduce_c(0)
     reduce_e(3)
     arrive(smc, u_core)
     both = sms[...] + smc[...]
@@ -695,10 +705,9 @@
     for d in range(1, Z):
         send(smx.at[0, (z + d) % Z], smz.at[d - 1], u_line, (replica, (z + d) % Z), o_line)
     for k in range(2):
-        reduce_m(4, k)
-    reduce_c(0)
-    for k in range(2):
         reduce_m(5, k)
+    for finish in early:
+        finish()
     reduce_d(2)
     reduce_c(4)
     reduce_d(1)

time: 165 us -> 164 us (level)
  no operation moved by 1% of the time
where the time goes in v5:
time: 164 us
  Pallas kernels  162 us (99%)
    pallas_call x1, Pallas kernels, local(): pl.pallas_call(kernel, out_shape=(shape(tile, BF16), shape(tile, BF16), s...  154 us
    pallas_call x1, Pallas kernels, local(): pl.pallas_call(finish_kernel, out_shape=(shape((128, 1024), BF16), shape(...  7.79 us

profile of v5, /device:TPU:0, one launch (start us, length us, event | category | flops | bytes accessed | tf_op | source)
XLA Modules:
  0.0 163.6 jit_solution(1359129788624361119)
XLA Ops:
  1.3 154.5 %shard_map.186 = (bf16[2,64,1024]{2,1,0:T(8,128)(2,1)}, bf16[2,64,1024]{2,1,0:T(8,128)(2,1)}, bf16[3,4,256,256]{3,2,1,0:T(8,128)(2,1)}, bf16[4,64,1024]{2,1,0:T(...) custom-call(bf16[2,64,1024]{2,1,0:T(8,128)(2,1)} %clips.1, ...), custom_call_target="tpu_custom_call" | custom-call | flops 10000000000 | bytes 33554432 | tf_op jit(solution)/shard_map/pallas_call | solution.py:860
  155.8 7.8 %shard_map.187 = (bf16[128,1024]{1,0:T(8,128)(2,1)}, f32[128,1024]{1,0:T(8,128)}, f32[256,3072]{1,0:T(8,128)}, f32[256,1024]{1,0:T(8,128)}, f32[256,4096]{1,0:T(...) custom-call(s32[1]{0:T(128)S(6)} %copy.21.live, ...), custom_call_target="tpu_custom_call" | custom-call | flops 4194304 | bytes 20971520 | tf_op jit(solution)/shard_map/pallas_call | solution.py:875

commit v6 on v5

--- a/solution.py
+++ b/solution.py
@@ -600,24 +600,20 @@
     for k in range(2):
         reduce_m(3, k)
     dh1[...] = res
+    gather_b(p_da)
     own(1, dn2 * xh2)
     own(3, dn2)
     own(6, da.astype(F32))
     fc1_sum = jnp.sum(dub[...].astype(F32).reshape(512, 1024), axis=0, keepdims=True)
     sms[pl.ds(9 + 2 * q, 1), :] = fc1_sum
 
-    gather_b(p_da)
     scatter_b(p_m)
     gather_c(p_da)
-    go[...] = mm_tn(ob[...].reshape(512, 256), dab[...].reshape(512, 1024)).astype(BF16).reshape(Z, HEAD, 1024)
-    reduce_a(1)
-
     def do_step(s, _):
         dob[s] = mm_nt(dab[s].reshape(256, 1024), wo[...].reshape(256, 1024)).astype(BF16)
         return 0
 
     lax.fori_loop(0, SLOTS, do_step, 0)
-    reduce_b(1)
 
     def attend_back(i, _):
         s = i // 2
@@ -644,6 +640,9 @@
     exchange(outb, out_k, e_out, backs)
     reduce_c(3)
     reduce_m(2, 1)
+    go[...] = mm_tn(ob[...].reshape(512, 256), dab[...].reshape(512, 1024)).astype(BF16).reshape(Z, HEAD, 1024)
+    reduce_a(1)
+
     lax.fori_loop(SLOTS, 2 * SLOTS, attend_back, 0)
 
     def dn1_step(zz, _):
@@ -654,6 +653,7 @@
         return 0
 
     lax.fori_loop(0, RANKS, dn1_step, 0)
+    reduce_b(1)
     scatter_a(p_d1)
     def dwq_step(zz, _):
         left = n1[:, :, :, strip(zz)].reshape(512, 256)
@@ -696,7 +696,6 @@
         reduce_m(4, k)
     reduce_c(1)
     reduce_c(0)
-    reduce_e(3)
     arrive(smc, u_core)
     both = sms[...] + smc[...]
     for zz in range(Z):
@@ -712,6 +711,7 @@
     reduce_c(4)
     reduce_d(1)
     reduce_c(5)
+    reduce_e(3)
     reduce_d(0)
     reduce_e(2)
     reduce_d(4)

time: 164 us -> 163 us (level)
  no operation moved by 1% of the time
where the time goes in v6:
time: 163 us
  Pallas kernels  161 us (99%)
    pallas_call x1, Pallas kernels, local(): pl.pallas_call(kernel, out_shape=(shape(tile, BF16), shape(tile, BF16), s...  153 us
    pallas_call x1, Pallas kernels, local(): pl.pallas_call(finish_kernel, out_shape=(shape((128, 1024), BF16), shape(...  7.79 us

profile of v6, /device:TPU:0, one launch (start us, length us, event | category | flops | bytes accessed | tf_op | source)
XLA Modules:
  0.0 162.7 jit_solution(6854285773341954957)
XLA Ops:
  1.3 153.5 %shard_map.186 = (bf16[2,64,1024]{2,1,0:T(8,128)(2,1)}, bf16[2,64,1024]{2,1,0:T(8,128)(2,1)}, bf16[3,4,256,256]{3,2,1,0:T(8,128)(2,1)}, bf16[4,64,1024]{2,1,0:T(...) custom-call(bf16[2,64,1024]{2,1,0:T(8,128)(2,1)} %clips.1, ...), custom_call_target="tpu_custom_call" | custom-call | flops 10000000000 | bytes 33554432 | tf_op jit(solution)/shard_map/pallas_call | solution.py:860
  154.8 7.8 %shard_map.187 = (bf16[128,1024]{1,0:T(8,128)(2,1)}, f32[128,1024]{1,0:T(8,128)}, f32[256,3072]{1,0:T(8,128)}, f32[256,1024]{1,0:T(8,128)}, f32[256,4096]{1,0:T(...) custom-call(s32[1]{0:T(128)S(6)} %copy.21.live, ...), custom_call_target="tpu_custom_call" | custom-call | flops 4194304 | bytes 20971520 | tf_op jit(solution)/shard_map/pallas_call | solution.py:875
